TPU v7x, 32 devices: a whole 2x2x4 slice. The times are simulated.
32 devices in a mesh: section: 4 (over y, x), ctx: 8 (over z, core).
Axes of the slice: x: 2, y: 2, z: 4, core: 2. Of those that a mesh axis runs over, the one named last changes fastest.
Arguments:
- queries: bfloat16 [4, 3072, 40, 128], P('section', 'ctx'), may hold values from -60 to 60
- keys_values: bfloat16 [3072, 2, 40, 128], P('ctx', None, 'section'), may hold values from -6 to 6
- positions: int32 [3072], P('ctx'), may hold values from 0 to 1533, as said below
- documents: int32 [3072], P('ctx'), may hold values from 0 to 3071, as said below
Outputs:
- attended: bfloat16 [4, 3072, 40, 128], P('section', 'ctx')
Inputs may be any that keep to these rules, and one draw needn't show every extreme that they name: `documents`: Non-decreasing along the sequence; each document is a run of 1 to 384 tokens sharing one id, one document has exactly 384 tokens, and the last document's id is 3071. `positions`: within a document the ids rise by 1 to 3 from each token to the next; a document's first id is 0 to 384.
All inputs are finite; a program needn't handle non-finite values.
Results may differ from a plain program's by a relative error of at most 0.01.
Values may be sent and summed in bfloat16 or wider, within the bound.
No kernel may reach another device: no remote copies, remote signals or barrier semaphores. Data moves between devices by JAX's collectives and lax.ppermute only.
A program may use at most 128 MiB of HBM per device.

v0:
```python
import jax
import jax.numpy as jnp
from jax import lax
from jax.sharding import PartitionSpec as P


def shifted(block, axis, distance):
    devices = range(lax.axis_size(axis))
    route = [(i - distance, i) for i in devices if i - distance in devices]
    return lax.ppermute(block, axis, route)


def rotate(values, token_positions):
    half_dim = values.shape[-1] // 2
    exponent = jnp.arange(half_dim, dtype=jnp.float32) * (2.0 / values.shape[-1])
    inverse = jnp.power(jnp.float32(10000.0), -exponent)
    angles = token_positions.astype(jnp.float32)[:, None] * inverse[None, :]
    cosine = jnp.cos(angles)[:, None, :]
    sine = jnp.sin(angles)[:, None, :]
    widened = values.astype(jnp.float32)
    lower = widened[..., :half_dim]
    upper = widened[..., half_dim:]
    joined = jnp.concatenate(
        [lower * cosine - upper * sine, upper * cosine + lower * sine], axis=-1
    )
    return joined.astype(jnp.bfloat16)


def attend(rotated, piece, key_docs, query_docs):
    query_rows = query_docs.shape[0]
    key_rows = key_docs.shape[0]
    head_count = piece.shape[2]
    head_dim = piece.shape[3]
    factor = max((option for option in range(1, 9) if head_count % option == 0))
    groups = head_count // factor

    def split_heads(values, length):
        return jnp.moveaxis(values.reshape(length, groups, factor, head_dim), 1, 0)

    allowed = jnp.logical_and(
        key_docs[None, :] == query_docs[:, None],
        jnp.arange(key_rows)[None, :] <= jnp.arange(query_rows)[:, None] + (key_rows - query_rows),
    )
    scale = head_dim ** (-0.5)

    def one_group(operands):
        query_part, key_part, value_part = operands
        scores = (
            jnp.einsum("qhd,khd->hqk", query_part, key_part, preferred_element_type=jnp.float32)
            * scale
        )
        scores = jnp.where(allowed[None], scores, -1e30)
        largest = jnp.max(scores, axis=-1, keepdims=True)
        weights = jnp.exp(scores - largest)
        probs = (weights / jnp.sum(weights, axis=-1, keepdims=True)).astype(jnp.bfloat16)
        mixed = jnp.einsum("hqk,khd->qhd", probs, value_part, preferred_element_type=jnp.float32)
        return mixed.astype(jnp.bfloat16)

    output = lax.map(
        one_group,
        (
            split_heads(rotated, query_rows),
            split_heads(piece[:, 0], key_rows),
            split_heads(piece[:, 1], key_rows),
        ),
    )
    return jnp.moveaxis(output, 0, 1).reshape(query_rows, head_count, head_dim)


def body(queries, keys_values, positions, documents):
    rotated = rotate(queries[0], positions)
    key_share = rotate(keys_values[:, 0], positions)
    share = jnp.stack([key_share, keys_values[:, 1]], axis=1)
    at_start = lax.axis_index("ctx") == 0
    whole = lax.all_gather(share, "section", axis=2, tiled=True)
    earlier, earlier_docs = shifted((whole, documents), "ctx", 1)
    key_docs = jnp.concatenate(
        [jnp.where(at_start, -1, earlier_docs).astype(jnp.int32), documents], axis=0
    )
    window = jnp.concatenate([earlier, whole], axis=0)
    result = attend(rotated, window, key_docs, documents)
    return result[None]


def solution(mesh):
    placed = (P("section", "ctx", None, None), P("ctx", None, "section", None), P("ctx"), P("ctx"))
    return jax.shard_map(
        body, mesh=mesh, in_specs=placed, out_specs=P("section", "ctx", None, None), check_vma=False
    )
```

profile of v0, /device:TPU:1, one launch (start us, length us, event | category | flops | bytes accessed | tf_op | source)
XLA Modules:
  0.0 325.4 jit_solution(8829666455155411308)
XLA Ops:
  7.2 6.4 %fusion.33 = (bf16[384,1,10,128]{3,1,2,0:T(2,128)(2,1)S(1)}, bf16[384,1,10,128]{3,1,2,0:T(2,128)(2,1)}) fusion(bf16[384,2,10,128]{3,1,2,0:T(2,128)(2,1)} %param.7), kind=kLoop, calls=%fused_computation.46 | loop fusion | bytes 3932160 | tf_op jit(solution)/shard_map/slice | solution.py:72
  15.2 3.8 %copy.21 = bf16[384,1,10,128]{0,3,2,1:T(8,128)(2,1)S(1)} copy(bf16[384,1,10,128]{3,1,2,0:T(2,128)(2,1)} %get-tuple-element.84) | data formatting | bytes 1966080
  21.2 85.5 %all-gather.2.cloned.1.call-done = bf16[384,2,40,128]{0,3,2,1:T(8,128)(2,1)} async-done(((bf16[384,2,10,128]{0,3,2,1:T(8,128)(2,1)}), bf16[384,2,40,128]{0,3,2,1:T(8,128)(2,1)}) %all-gather.2.cloned.1.call-update) | async-done | bytes 7864336 | tf_op jit(solution)/shard_map/all_gather | solution.py:75
  106.7 3.7 %collective-permute-start = (bf16[384,2,40,128]{0,3,2,1:T(8,128)(2,1)}, bf16[384,2,40,128]{0,3,2,1:T(8,128)(2,1)}, u32[]{:S(2)}, u32[]{:S(2)}) collective-permute-start(bf16[384,2,40,128]{0,3,2,1:T(8,128)(2,1)} %all-gather.2.cloned.1.call-done), channel_id=1, source_target_pairs={{0,1},{1,2},{2,3},{3,4},{4,5},{5,6},{6,7},{8,9},{9,10},{10,11},{11... | collective-permute-start | bytes 23592968 | tf_op jit(solution)/shard_map/ppermute | solution.py:10
  119.7 4.1 %maximum_bitcast_fusion = bf16[5,384,8,128]{3,1,2,0:T(8,128)(2,1)} fusion(bf16[384,5,8,64]{3,0,2,1:T(8,128)(2,1)S(1)} %bitcast.53, bf16[384,5,8,64]{3,0,2,1:T(8,128)(2,1)S(1)} %bitcast.52), kind=kLoop, calls=%fused_computation.28 | loop fusion | flops 7864320 | bytes 7864320 | tf_op jit(solution)/shard_map/transpose | solution.py:38
  123.8 71.6 %collective-permute-done.1 = s32[384]{0:T(512)S(1)} collective-permute-done((s32[384]{0:T(512)S(1)}, s32[384]{0:T(512)S(1)}, u32[]{:S(2)}, u32[]{:S(2)}) %collective-permute-start.1) | collective-permute-done | bytes 1568 | tf_op jit(solution)/shard_map/ppermute | solution.py:10
  195.5 8.1 %constant_dynamic-update-slice_fusion.1 = bf16[768,2,40,128]{0,3,2,1:T(8,128)(2,1)} fusion(bf16[384,2,40,128]{0,3,2,1:T(8,128)(2,1)} %collective-permute-done), kind=kLoop, calls=%fused_computation.39 | loop fusion | bytes 15728640
  203.6 4.3 %constant_dynamic-update-slice_fusion = bf16[768,2,40,128]{0,3,2,1:T(8,128)(2,1)} fusion(bf16[768,2,40,128]{0,3,2,1:T(8,128)(2,1)} %constant_dynamic-update-slice_fusion.1, bf16[384,2,40,128]{0,3,2,1:T(8,128)(2,1)S(1)} %bitcast.55), kind=kLoop, calls=%fused_computation.38 | loop fusion | bytes 15728640 | tf_op jit(solution)/shard_map/concatenate | solution.py:80
  207.9 11.1 %fusion.32 = (bf16[768,1,40,128]{0,3,2,1:T(8,128)(2,1)}, bf16[768,1,40,128]{0,3,2,1:T(8,128)(2,1)}) fusion(bf16[768,2,40,128]{0,3,2,1:T(8,128)(2,1)} %constant_dynamic-update-slice_fusion), kind=kLoop, calls=%fused_computation.45 | loop fusion | bytes 31457280 | tf_op jit(solution)/shard_map/slice | solution.py:63
  219.0 10.6 %copy.18 = bf16[768,5,8,128]{3,0,2,1:T(8,128)(2,1)} copy(bf16[768,5,8,128]{0,3,2,1:T(8,128)(2,1)} %bitcast.51) | data formatting | bytes 15728640 | tf_op jit(solution)/shard_map/reshape;squeeze | solution.py:38
  229.7 82.5 %while.11 = (s32[]{:T(128)}, bf16[5,384,8,128]{1,3,2,0:T(8,128)(2,1)}, bf16[5,768,8,128]{1,3,2,0:T(8,128)(2,1)}, bf16[5,384,8,128]{3,1,2,0:T(8,128)(2,1)}, bf16[...) while((s32[]{:T(128)}, ...), condition=%wide.region_3.4_spmd.clone, body=%wide.region_0.3_spmd.clone.sunk | while | flops 1228112640 | bytes 43090012 | solution.py:59
  233.1 6.5 %fusion.46 = (f32[8,384]{1,0:T(8,128)S(1)}, f32[8,384,768]{2,1,0:T(8,128)}) fusion(f32[8,384,768]{2,1,0:T(8,128)S(1)} %fusion.44, pred[384,768]{1,0:T(8,128)(4,1)S(1)} %fusion.45), kind=kOutput, calls=%fused_computation.44.clone.1 | output fusion | flops 14156543 | bytes 19181568 | tf_op jit(solution)/shard_map/while/body/eval_jaxpr/sub | solution.py:54
  239.6 6.6 %fusion.47 = bf16[5,384,8,128]{1,3,2,0:T(8,128)(2,1)} fusion(bf16[5,384,8,128]{1,3,2,0:T(8,128)(2,1)} %get-tuple-element.150, s32[]{:T(128)} %get-tuple-element.149, f32[8,384,768]{2,1,0:T(8,128)} %get-tuple-element.138, f32[8,384]{1,0:T(8,128)S(1)} %get-tuple-element.139, bf16[5,768,8,128]{1,3,2,0:T(8,128)(2,1)} %get-tuple-element.160), kind=kOutput, calls=%fused_computation.17.clone.1 | convolution fusion | flops 609091584 | bytes 11809792 | tf_op jit(solution)/shard_map/while/body/eval_jaxpr/hqk,khd->qhd/dot_general | solution.py:56
  246.2 3.0 fusion.44
  249.6 6.5 %fusion.46 = (f32[8,384]{1,0:T(8,128)S(1)}, f32[8,384,768]{2,1,0:T(8,128)}) fusion(f32[8,384,768]{2,1,0:T(8,128)S(1)} %fusion.44, pred[384,768]{1,0:T(8,128)(4,1)S(1)} %fusion.45), kind=kOutput, calls=%fused_computation.44.clone.1 | output fusion | flops 14156543 | bytes 19181568 | tf_op jit(solution)/shard_map/while/body/eval_jaxpr/sub | solution.py:54
  256.1 6.6 %fusion.47 = bf16[5,384,8,128]{1,3,2,0:T(8,128)(2,1)} fusion(bf16[5,384,8,128]{1,3,2,0:T(8,128)(2,1)} %get-tuple-element.150, s32[]{:T(128)} %get-tuple-element.149, f32[8,384,768]{2,1,0:T(8,128)} %get-tuple-element.138, f32[8,384]{1,0:T(8,128)S(1)} %get-tuple-element.139, bf16[5,768,8,128]{1,3,2,0:T(8,128)(2,1)} %get-tuple-element.160), kind=kOutput, calls=%fused_computation.17.clone.1 | convolution fusion | flops 609091584 | bytes 11809792 | tf_op jit(solution)/shard_map/while/body/eval_jaxpr/hqk,khd->qhd/dot_general | solution.py:56
  262.7 3.0 fusion.44
  266.1 6.5 %fusion.46 = (f32[8,384]{1,0:T(8,128)S(1)}, f32[8,384,768]{2,1,0:T(8,128)}) fusion(f32[8,384,768]{2,1,0:T(8,128)S(1)} %fusion.44, pred[384,768]{1,0:T(8,128)(4,1)S(1)} %fusion.45), kind=kOutput, calls=%fused_computation.44.clone.1 | output fusion | flops 14156543 | bytes 19181568 | tf_op jit(solution)/shard_map/while/body/eval_jaxpr/sub | solution.py:54
  272.6 6.5 %fusion.47 = bf16[5,384,8,128]{1,3,2,0:T(8,128)(2,1)} fusion(bf16[5,384,8,128]{1,3,2,0:T(8,128)(2,1)} %get-tuple-element.150, s32[]{:T(128)} %get-tuple-element.149, f32[8,384,768]{2,1,0:T(8,128)} %get-tuple-element.138, f32[8,384]{1,0:T(8,128)S(1)} %get-tuple-element.139, bf16[5,768,8,128]{1,3,2,0:T(8,128)(2,1)} %get-tuple-element.160), kind=kOutput, calls=%fused_computation.17.clone.1 | convolution fusion | flops 609091584 | bytes 11809792 | tf_op jit(solution)/shard_map/while/body/eval_jaxpr/hqk,khd->qhd/dot_general | solution.py:56
  282.5 6.5 %fusion.46 = (f32[8,384]{1,0:T(8,128)S(1)}, f32[8,384,768]{2,1,0:T(8,128)}) fusion(f32[8,384,768]{2,1,0:T(8,128)S(1)} %fusion.44, pred[384,768]{1,0:T(8,128)(4,1)S(1)} %fusion.45), kind=kOutput, calls=%fused_computation.44.clone.1 | output fusion | flops 14156543 | bytes 19181568 | tf_op jit(solution)/shard_map/while/body/eval_jaxpr/sub | solution.py:54
  289.0 6.7 %fusion.47 = bf16[5,384,8,128]{1,3,2,0:T(8,128)(2,1)} fusion(bf16[5,384,8,128]{1,3,2,0:T(8,128)(2,1)} %get-tuple-element.150, s32[]{:T(128)} %get-tuple-element.149, f32[8,384,768]{2,1,0:T(8,128)} %get-tuple-element.138, f32[8,384]{1,0:T(8,128)S(1)} %get-tuple-element.139, bf16[5,768,8,128]{1,3,2,0:T(8,128)(2,1)} %get-tuple-element.160), kind=kOutput, calls=%fused_computation.17.clone.1 | convolution fusion | flops 609091584 | bytes 11809792 | tf_op jit(solution)/shard_map/while/body/eval_jaxpr/hqk,khd->qhd/dot_general | solution.py:56
  299.1 6.5 %fusion.46 = (f32[8,384]{1,0:T(8,128)S(1)}, f32[8,384,768]{2,1,0:T(8,128)}) fusion(f32[8,384,768]{2,1,0:T(8,128)S(1)} %fusion.44, pred[384,768]{1,0:T(8,128)(4,1)S(1)} %fusion.45), kind=kOutput, calls=%fused_computation.44.clone.1 | output fusion | flops 14156543 | bytes 19181568 | tf_op jit(solution)/shard_map/while/body/eval_jaxpr/sub | solution.py:54
  305.6 6.6 %fusion.47 = bf16[5,384,8,128]{1,3,2,0:T(8,128)(2,1)} fusion(bf16[5,384,8,128]{1,3,2,0:T(8,128)(2,1)} %get-tuple-element.150, s32[]{:T(128)} %get-tuple-element.149, f32[8,384,768]{2,1,0:T(8,128)} %get-tuple-element.138, f32[8,384]{1,0:T(8,128)S(1)} %get-tuple-element.139, bf16[5,768,8,128]{1,3,2,0:T(8,128)(2,1)} %get-tuple-element.160), kind=kOutput, calls=%fused_computation.17.clone.1 | convolution fusion | flops 609091584 | bytes 11809792 | tf_op jit(solution)/shard_map/while/body/eval_jaxpr/hqk,khd->qhd/dot_general | solution.py:56
  312.2 6.4 %copy.19 = bf16[384,5,8,128]{3,2,1,0:T(8,128)(2,1)} copy(bf16[384,5,8,128]{0,3,2,1:T(8,128)(2,1)} %bitcast.13) | data formatting | bytes 7864320 | tf_op jit(solution)/shard_map/transpose | solution.py:67
  (36 shorter events, 24.7 us)
Async XLA Ops:
  6.5 100.2 %all-gather.2.cloned.1.call-start = ((), (), s32[]{:S(2)}) async-start(), calls=%async_computation | async-start | bytes 9830400 | tf_op jit(solution)/shard_map/all_gather | solution.py:75
  15.0 95.3 %copy-start = (s32[384]{0:T(512)S(1)}, s32[384]{0:T(512)}, u32[]{:S(2)}) copy-start(s32[384]{0:T(512)} %param.9) | copy-start | bytes 4612
  106.7 88.8 %collective-permute-start = (bf16[384,2,40,128]{0,3,2,1:T(8,128)(2,1)}, bf16[384,2,40,128]{0,3,2,1:T(8,128)(2,1)}, u32[]{:S(2)}, u32[]{:S(2)}) collective-permute-start(bf16[384,2,40,128]{0,3,2,1:T(8,128)(2,1)} %all-gather.2.cloned.1.call-done), channel_id=1, source_target_pairs={{0,1},{1,2},{2,3},{3,4},{4,5},{5,6},{6,7},{8,9},{9,10},{10,11},{11... | collective-permute-start | bytes 23592968 | tf_op jit(solution)/shard_map/ppermute | solution.py:10
  110.4 85.1 %collective-permute-start.1 = (s32[384]{0:T(512)S(1)}, s32[384]{0:T(512)S(1)}, u32[]{:S(2)}, u32[]{:S(2)}) collective-permute-start(s32[384]{0:T(512)S(1)} %copy-done), channel_id=1, source_target_pairs={{0,1},{1,2},{2,3},{3,4},{4,5},{5,6},{6,7},{8,9},{9,10},{10,11},{11... | collective-permute-start | bytes 4616 | tf_op jit(solution)/shard_map/ppermute | solution.py:10
  195.5 8.1 %slice-start = ((s8[7864320]{0:T(1024)(128)(4,1)}), s8[4194304]{0:T(1024)(128)(4,1)S(1)}, s32[]{:S(2)}) async-start(s8[7864320]{0:T(1024)(128)(4,1)} %bitcast.54), calls=%async_computation.1 | async-start | bytes 8388608
  195.5 8.1 %slice-start.1 = ((s8[7864320]{0:T(1024)(128)(4,1)}), s8[3670016]{0:T(1024)(128)(4,1)S(1)}, s32[]{:S(2)}) async-start(s8[7864320]{0:T(1024)(128)(4,1)} %bitcast.54), calls=%async_computation.2 | async-start | bytes 7340032
Sparse Core Ops, SparseCore 0:
  21.3 85.3 all-gather.1
where the time goes:
time: 326 us; the launch traced here: 325 us
  waiting for transfers between devices  157 us (48%)
  local copies, waits for them, and re-layouts  54.2 us (17%)
  matrix products  48.2 us (15%)
  other arithmetic  46.6 us (14%)
  between operations  13.5 us (4%)
  starting transfers between devices  5.59 us (2%)
    all_gather x1, waiting for transfers between devices, body(): whole = lax.all_gather(share, 'section', axis=2, tiled=True)  85.5 us
    ppermute x2, waiting for transfers between devices, shifted(): return lax.ppermute(block, axis, route)  71.6 us
    dot_general x5, matrix products, one_group(): jnp.einsum('hqk,khd->qhd', probs, value_part, preferred_element_type=jnp....  33 us
    sub x5, other arithmetic, one_group(): weights = jnp.exp(scores - largest)  32.5 us
    dot_general x5, matrix products, one_group(): jnp.einsum('qhd,khd->hqk', query_part, key_part, preferred_element_type=j...  15.2 us
    unnamed x9, local copies, waits for them, and re-layouts  13.3 us
    slice x1, local copies, waits for them, and re-layouts, attend(): piece[:, 0]  11.1 us
    another operation x1, local copies, waits for them, and re-layouts, split_heads(): return jnp.moveaxis(values.reshape(length, groups, factor, head_dim), 1, 0)  10.6 us
  transfers between devices with their start and end apart: 3, of which 2 were waited for; matrix products, arithmetic and copies ran while one was open for 4% of the time, Pallas kernels for 0%

commit v1 on v0

v1 whole, which is shorter than its diff:
```python
import functools

import jax
import jax.numpy as jnp
import numpy as np
from jax import lax
from jax.experimental import pallas as pl
from jax.experimental.pallas import tpu as pltpu
from jax.sharding import PartitionSpec as P

ACROSS_X = ((0, 1), (1, 0), (2, 3), (3, 2))
ACROSS_Y = ((0, 2), (2, 0), (1, 3), (3, 1))
BLOCK = 128
PARAMS = pltpu.CompilerParams(vmem_limit_bytes=48 * 2**20)
NT = (((1,), (1,)), ((), ()))


def shifted(block, axis, distance):
    devices = range(lax.axis_size(axis))
    route = [(i - distance, i) for i in devices if i - distance in devices]
    return lax.ppermute(block, axis, route)


def angle_tables(token_positions, head_dim):
    half_dim = head_dim // 2
    exponent = jnp.arange(half_dim, dtype=jnp.float32) * (2.0 / head_dim)
    inverse = jnp.power(jnp.float32(10000.0), -exponent)
    angles = token_positions.astype(jnp.float32)[:, None] * inverse[None, :]
    cosine = jnp.cos(angles)
    sine = jnp.sin(angles)
    return jnp.concatenate([cosine, cosine], axis=1), jnp.concatenate([-sine, sine], axis=1)


def turn(values, cosine, sine):
    return (values * cosine + pltpu.roll(values, values.shape[-1] // 2, 1) * sine).astype(jnp.bfloat16)


def prepare_cache(keys_values, cosine, sine):
    tokens, _, heads, head_dim = keys_values.shape
    half = heads // 2
    step = BLOCK
    rows = jnp.transpose(keys_values, (0, 2, 1, 3)).reshape(tokens * heads * 2, head_dim)

    def kernel(rows_ref, cosine_ref, sine_ref, all_ref, a_ref, b_ref, wide):
        wide[...] = rows_ref[...].astype(jnp.float32)
        for head in range(heads):
            key = wide[pl.ds(2 * head, step, stride=2 * heads), :]
            key = turn(key, cosine_ref[...], sine_ref[...])
            value = wide[pl.ds(2 * head + 1, step, stride=2 * heads), :].astype(jnp.bfloat16)
            part = a_ref if head < half else b_ref
            all_ref[0, head] = key
            all_ref[1, head] = value
            part[0, head % half] = key
            part[1, head % half] = value

    table = pl.BlockSpec((step, head_dim), lambda i: (i, 0))
    counts = (heads, half, heads - half)
    return pl.pallas_call(
        kernel,
        grid=(tokens // step,),
        in_specs=[pl.BlockSpec((step * heads * 2, head_dim), lambda i: (i, 0)), table, table],
        out_specs=[pl.BlockSpec((2, n, step, head_dim), lambda i: (0, 0, i, 0)) for n in counts],
        out_shape=[jax.ShapeDtypeStruct((2, n, tokens, head_dim), jnp.bfloat16) for n in counts],
        scratch_shapes=[pltpu.VMEM((step * heads * 2, head_dim), jnp.float32)],
        compiler_params=PARAMS,
        name="prepare_cache",
    )(rows, cosine, sine)


def prepare_queries(queries, cosine, sine, starts, counts):
    tokens, heads, head_dim = queries.shape
    step = BLOCK

    def kernel(starts_ref, queries_ref, cosine_ref, sine_ref, *refs):
        wide = refs[-1]
        wide[...] = queries_ref[...].reshape(step * heads, head_dim).astype(jnp.float32)
        run = 0
        for out_ref, runs in zip(refs[:-1], counts):
            slot = 0
            for count in runs:
                for i in range(count):
                    head = wide[pl.ds(starts_ref[run] + i, step, stride=heads), :]
                    out_ref[slot] = turn(head, cosine_ref[...], sine_ref[...])
                    slot += 1
                run += 1

    table = pl.BlockSpec((step, head_dim), lambda i, s: (i, 0))
    totals = [sum(runs) for runs in counts]
    return pl.pallas_call(
        kernel,
        grid_spec=pltpu.PrefetchScalarGridSpec(
            num_scalar_prefetch=1,
            grid=(tokens // step,),
            in_specs=[pl.BlockSpec((step, heads, head_dim), lambda i, s: (i, 0, 0)), table, table],
            out_specs=[pl.BlockSpec((n, step, head_dim), lambda i, s: (0, i, 0)) for n in totals],
            scratch_shapes=[pltpu.VMEM((step * heads, head_dim), jnp.float32)],
        ),
        out_shape=[jax.ShapeDtypeStruct((n, tokens, head_dim), jnp.bfloat16) for n in totals],
        compiler_params=PARAMS,
        name="prepare_queries",
    )(starts, queries, cosine, sine)


def mask_bias(documents, earlier_docs):
    tokens = documents.shape[0]
    window = jnp.concatenate([earlier_docs, documents])
    blocks = tokens // BLOCK
    width = tokens + BLOCK
    keys = jnp.stack([window[BLOCK * r : BLOCK * r + width] for r in range(blocks)])
    rows = documents.reshape(blocks, BLOCK)
    causal = jnp.arange(width)[None, :] <= jnp.arange(BLOCK)[:, None] + tokens
    allowed = jnp.logical_and(keys[:, None, :] == rows[:, :, None], causal[None])
    return jnp.where(allowed, 0.0, -1e30).astype(jnp.float32)


def attend(queries, current, earlier, bias):
    count = queries[0][2]
    tokens, head_dim = queries[0][0].shape[-2:]
    blocks = tokens // BLOCK
    scale = float(head_dim**-0.5 * np.log2(np.e))

    def kernel(qa, qb, ca, cb, ea, eb, bias_ref, oa, ob):
        for q, c, e, o in ((qa, ca, ea, oa), (qb, cb, eb, ob)):
            for r in range(blocks):
                low, high = BLOCK * r, BLOCK * (r + 1)
                key = jnp.concatenate([e[0, 0, low:], c[0, 0, :high]], axis=0)
                value = jnp.concatenate([e[1, 0, low:], c[1, 0, :high]], axis=0)
                scores = lax.dot_general(q[0, low:high], key, NT, preferred_element_type=jnp.float32)
                scores = scores + bias_ref[r]
                largest = jnp.max(scores, axis=1, keepdims=True) * scale
                weights = jnp.exp2(scores * scale - largest).astype(jnp.bfloat16)
                extended = jnp.concatenate([value, jnp.ones_like(value)], axis=1)
                mixed = jnp.dot(weights, extended, preferred_element_type=jnp.float32)
                o[0, low:high] = (mixed[:, :head_dim] / mixed[:, head_dim:]).astype(jnp.bfloat16)

    def one(first):
        return pl.BlockSpec((1, tokens, head_dim), lambda i: (i + first, 0, 0))

    def pair(first):
        return pl.BlockSpec((2, 1, tokens, head_dim), lambda i: (0, i + first, 0, 0))

    operands = [*queries, *current, *earlier]
    in_specs = [one(o[1]) for o in queries] + [pair(o[1]) for o in (*current, *earlier)]
    in_specs.append(pl.BlockSpec(bias.shape, lambda i: (0, 0, 0)))
    return pl.pallas_call(
        kernel,
        grid=(count,),
        in_specs=in_specs,
        out_specs=[one(0)] * 2,
        out_shape=[jax.ShapeDtypeStruct((count, tokens, head_dim), jnp.bfloat16)] * 2,
        compiler_params=PARAMS,
        cost_estimate=pl.CostEstimate(
            flops=2 * count * 2 * blocks * BLOCK * (tokens + BLOCK) * head_dim * 2,
            bytes_accessed=2 * count * 6 * tokens * head_dim * 2,
            transcendentals=2 * count * blocks * BLOCK * (tokens + BLOCK),
        ),
        name="attend",
    )(*[o[0] for o in operands], bias)


def assemble(pieces, slots):
    count, tokens, head_dim = pieces[0].shape
    heads = count * len(pieces)
    step = BLOCK

    def kernel(slots_ref, *refs):
        *piece_refs, out_ref, gathered = refs
        for p, ref in enumerate(piece_refs):
            gathered[pl.ds(slots_ref[p] * count, count)] = ref[...]
        out_ref[...] = jnp.swapaxes(gathered[...], 0, 1)

    return pl.pallas_call(
        kernel,
        grid_spec=pltpu.PrefetchScalarGridSpec(
            num_scalar_prefetch=1,
            grid=(tokens // step,),
            in_specs=[pl.BlockSpec((count, step, head_dim), lambda i, s: (0, i, 0))] * len(pieces),
            out_specs=pl.BlockSpec((step, heads, head_dim), lambda i, s: (i, 0, 0)),
            scratch_shapes=[pltpu.VMEM((heads, step, head_dim), jnp.bfloat16)],
        ),
        out_shape=jax.ShapeDtypeStruct((tokens, heads, head_dim), jnp.bfloat16),
        compiler_params=PARAMS,
        name="assemble",
    )(slots, *pieces)


def across(value, route):
    return lax.ppermute(value, "section", route)


def square_body(queries, keys_values, positions, documents):
    head_dim = queries.shape[-1]
    mine = keys_values.shape[2]
    half = mine // 2
    section = lax.axis_index("section")
    beside_x, beside_y, opposite = section ^ 1, section ^ 2, section ^ 3
    earlier_docs = shifted(documents, "ctx", 1)
    earlier_docs = jnp.where(lax.axis_index("ctx") == 0, -1, earlier_docs)

    cosine, sine = angle_tables(positions, head_dim)
    share, share_a, share_b = prepare_cache(keys_values, cosine, sine)
    cache_a = across(share_a, ACROSS_X)
    cache_b = across(share_b, ACROSS_Y)
    earlier = shifted(share, "ctx", 1)

    starts = jnp.stack(
        [
            beside_y * mine,
            beside_x * mine + half,
            opposite * mine,
            opposite * mine + half,
            section * mine,
            beside_x * mine,
            beside_y * mine + half,
        ]
    ).astype(jnp.int32)
    near_y, near_x, far_y, far_x, own_near, own_far = prepare_queries(
        queries[0], cosine, sine, starts, ((half,), (half,), (half,), (half,), (mine,), (half, half))
    )
    bias = mask_bias(documents, earlier_docs)
    near_a = across(near_y, ACROSS_Y)
    near_b = across(near_x, ACROSS_X)
    far_a = across(far_y, ACROSS_Y)
    far_b = across(far_x, ACROSS_X)
    earlier_a = shifted(cache_a, "ctx", 1)
    earlier_b = shifted(cache_b, "ctx", 1)

    near_cache = ((share, 0), (share, half))
    near_earlier = ((earlier, 0), (earlier, half))
    far_cache = ((cache_a, 0), (cache_b, 0))
    far_earlier = ((earlier_a, 0), (earlier_b, 0))
    out_near_a, out_near_b = attend(((near_a, 0, half), (near_b, 0, half)), near_cache, near_earlier, bias)
    back_near_a = across(out_near_a, ACROSS_Y)
    back_near_b = across(out_near_b, ACROSS_X)
    out_far_a, out_far_b = attend(((far_a, 0, half), (far_b, 0, half)), far_cache, far_earlier, bias)
    back_far_a = across(out_far_a, ACROSS_Y)
    back_far_b = across(out_far_b, ACROSS_X)
    own_near_a, own_near_b = attend(((own_near, 0, half), (own_near, half, half)), near_cache, near_earlier, bias)
    own_far_a, own_far_b = attend(((own_far, 0, half), (own_far, half, half)), far_cache, far_earlier, bias)

    slots = jnp.stack(
        [
            2 * section,
            2 * section + 1,
            2 * beside_x,
            2 * beside_y + 1,
            2 * beside_y,
            2 * beside_x + 1,
            2 * opposite,
            2 * opposite + 1,
        ]
    ).astype(jnp.int32)
    pieces = (own_near_a, own_near_b, own_far_a, own_far_b, back_near_a, back_near_b, back_far_a, back_far_b)
    return assemble(pieces, slots)[None]


def general_body(queries, keys_values, positions, documents):
    tokens, heads, head_dim = queries.shape[1:]
    mine = keys_values.shape[2]
    cosine, sine = angle_tables(positions, head_dim)
    earlier_docs = shifted(documents, "ctx", 1)
    earlier_docs = jnp.where(lax.axis_index("ctx") == 0, -1, earlier_docs)
    share = prepare_cache(keys_values, cosine, sine)[0]
    whole = lax.all_gather(share, "section", axis=1, tiled=True)
    earlier = shifted(whole, "ctx", 1)
    starts = jnp.zeros((1,), jnp.int32)
    (rotated,) = prepare_queries(queries[0], cosine, sine, starts, ((heads,),))
    bias = mask_bias(documents, earlier_docs)
    half = heads // 2
    outs = attend(
        ((rotated, 0, half), (rotated, half, half)),
        ((whole, 0), (whole, half)),
        ((earlier, 0), (earlier, half)),
        bias,
    )
    return assemble(outs, jnp.arange(2, dtype=jnp.int32))[None]


def solution(mesh):
    placed = (P("section", "ctx", None, None), P("ctx", None, "section", None), P("ctx"), P("ctx"))
    body = square_body if mesh.shape["section"] == 4 else general_body
    return jax.shard_map(
        body, mesh=mesh, in_specs=placed, out_specs=P("section", "ctx", None, None), check_vma=False
    )
```

time: 326 us -> 99.4 us (0.30)
  waiting for transfers between devices: 157 us -> 28.8 us
  local copies, waits for them, and re-layouts: 54.2 us -> 5.12 us
  matrix products: 48.2 us -> 0 us
  other arithmetic: 46.6 us -> 1.96 us
  Pallas kernels: 0 us -> 40.8 us
  starting transfers between devices: 5.59 us -> 20.8 us
  between operations: 13.5 us -> 0.2 us
    all_gather x1 -> x0, waiting for transfers between devices: 85.5 us -> none  [body(): whole = lax.all_gather(share, 'section', axis=2, tiled=True)]
    dot_general x10 -> x0, matrix products: 48.2 us -> none  [the longest x5 33 us: one_group(): jnp.einsum('hqk,khd->qhd', probs, value_part, preferred_element_type=jnp....]
    ppermute x2 -> x4, waiting for transfers between devices: 71.6 us -> 28.5 us  [shifted(): return lax.ppermute(block, axis, route)]
    pallas_call x0 -> x7, Pallas kernels: none -> 40.8 us  [the longest x4 25.2 us: attend(): pl.pallas_call(kernel, grid=(count,), in_specs=in_specs, out_specs=[one(0...]
    sub x5 -> x0, other arithmetic: 32.5 us -> none  [one_group(): weights = jnp.exp(scores - largest)]
    slice x2 -> x1, local copies, waits for them, and re-layouts: 17.5 us -> 0.01 us  [mask_bias(): window[BLOCK * r:BLOCK * r + width]]
    another operation x3 -> x2, local copies, waits for them, and re-layouts: 12.5 us -> 0.17 us  [the longest x1 0.09 us: square_body(): jnp.stack([beside_y * mine, beside_x * mine + half, opposite * mine, oppo...]
    unnamed x9 -> x14, local copies, waits for them, and re-layouts: 13.3 us -> 4.94 us
  transfers between devices with their start and end apart: 3 -> 14, of which waited for: 2 -> 4; matrix products, arithmetic and copies ran while one was open for 4% -> 1% of each run, Pallas kernels for 0% -> 32%
where the time goes in v1:
time: 99.4 us; the launch traced here: 97.7 us
  Pallas kernels  40.8 us (41%)
  waiting for transfers between devices  28.8 us (29%)
  starting transfers between devices  20.8 us (21%)
  local copies, waits for them, and re-layouts  5.12 us (5%)
  other arithmetic  1.96 us (2%)
    ppermute x4, waiting for transfers between devices, shifted(): return lax.ppermute(block, axis, route)  28.5 us
    pallas_call x4, Pallas kernels, attend(): pl.pallas_call(kernel, grid=(count,), in_specs=in_specs, out_specs=[one(0...  25.2 us
    ppermute x4, starting transfers between devices, shifted(): return lax.ppermute(block, axis, route)  12.9 us
    ppermute x10, starting transfers between devices, across(): return lax.ppermute(value, 'section', route)  7.91 us
    pallas_call x1, Pallas kernels, prepare_queries(): pl.pallas_call(kernel, grid_spec=pltpu.PrefetchScalarGridSpec(num_scalar_...  6.18 us
    pallas_call x1, Pallas kernels, assemble(): pl.pallas_call(kernel, grid_spec=pltpu.PrefetchScalarGridSpec(num_scalar_...  5.32 us
    unnamed x14, local copies, waits for them, and re-layouts  4.94 us
    pallas_call x1, Pallas kernels, prepare_cache(): pl.pallas_call(kernel, grid=(tokens // step,), in_specs=[pl.BlockSpec((st...  4.14 us
  transfers between devices with their start and end apart: 14, of which 4 were waited for; matrix products, arithmetic and copies ran while one was open for 1% of the time, Pallas kernels for 32%

profile of v1, /device:TPU:1, one launch (start us, length us, event | category | flops | bytes accessed | tf_op | source)
XLA Modules:
  0.0 97.7 jit_solution(3238380425076625994)
XLA Ops:
  1.6 4.1 %prepare_cache.1 = (bf16[2,10,384,128]{3,2,1,0:T(8,128)(2,1)S(1)}, bf16[2,5,384,128]{3,2,1,0:T(8,128)(2,1)}, bf16[2,5,384,128]{3,2,1,0:T(8,128)(2,1)}) custom-call(bf16[7680,128]{1,0:T(8,128)(2,1)} %bitcast.25, f32[384,128]{1,0:T(8,128)S(1)} %get-tuple-element.45.cosine_ref, f32[384,128]{1,0:T(8,128)S(1)} %get-tuple-element.46.sine_ref), custom_call_target="tpu_custom_call" | custom-call | tf_op jit(solution)/shard_map/prepare_cache/pallas_call | solution.py:58
  5.8 2.0 %collective-permute-start.2 = (bf16[2,5,384,128]{3,2,1,0:T(8,128)(2,1)}, bf16[2,5,384,128]{3,2,1,0:T(8,128)(2,1)}, u32[]{:S(2)}, u32[]{:S(2)}) collective-permute-start(bf16[2,5,384,128]{3,2,1,0:T(8,128)(2,1)} %get-tuple-element.27), channel_id=1, source_target_pairs={{0,8},{8,0},{16,24},{24,16},{1,9},{9,1},{17,25},{25,17},{2,10},{10... | collective-permute-start | bytes 2949128 | tf_op jit(solution)/shard_map/ppermute | solution.py:188
  7.8 1.2 %collective-permute-start.3 = (bf16[2,5,384,128]{3,2,1,0:T(8,128)(2,1)}, bf16[2,5,384,128]{3,2,1,0:T(8,128)(2,1)}, u32[]{:S(2)}, u32[]{:S(2)}) collective-permute-start(bf16[2,5,384,128]{3,2,1,0:T(8,128)(2,1)} %get-tuple-element.28), channel_id=1, source_target_pairs={{0,16},{16,0},{8,24},{24,8},{1,17},{17,1},{9,25},{25,9},{2,18},{18... | collective-permute-start | bytes 2949128 | tf_op jit(solution)/shard_map/ppermute | solution.py:188
  9.1 4.3 %collective-permute-start = (bf16[2,10,384,128]{3,2,1,0:T(8,128)(2,1)S(1)}, bf16[2,10,384,128]{3,2,1,0:T(8,128)(2,1)}, u32[]{:S(2)}, u32[]{:S(2)}) collective-permute-start(bf16[2,10,384,128]{3,2,1,0:T(8,128)(2,1)S(1)} %get-tuple-element.23.ca.cb), channel_id=1, source_target_pairs={{0,1},{1,2},{2,3},{3,4},{4,5},{5,6},{6,7},{8,9},{9,10},{10,11},{11... | collective-permute-start | bytes 5898248 | tf_op jit(solution)/shard_map/ppermute | solution.py:21
  13.4 1.9 %collective-permute-start.1 = (s32[384]{0:T(512)S(1)}, s32[384]{0:T(512)S(1)}, u32[]{:S(2)}, u32[]{:S(2)}) collective-permute-start(s32[384]{0:T(512)S(1)} %copy-done.6), channel_id=1, source_target_pairs={{0,1},{1,2},{2,3},{3,4},{4,5},{5,6},{6,7},{8,9},{9,10},{10,11},{11... | collective-permute-start | bytes 4616 | tf_op jit(solution)/shard_map/ppermute | solution.py:21
  15.4 6.2 %prepare_queries.1 = (bf16[5,384,128]{2,1,0:T(8,128)(2,1)}, bf16[5,384,128]{2,1,0:T(8,128)(2,1)}, bf16[5,384,128]{2,1,0:T(8,128)(2,1)}, bf16[5,384,128]{2,1,0:T(...) custom-call(s32[7]{0:T(128)S(1)} %stack.79.starts_ref, ...), custom_call_target="tpu_custom_call" | custom-call | tf_op jit(solution)/shard_map/prepare_queries/pallas_call | solution.py:89
  21.6 1.0 %copy-done = bf16[10,384,128]{2,1,0:T(8,128)(2,1)} copy-done((bf16[10,384,128]{2,1,0:T(8,128)(2,1)}, bf16[10,384,128]{2,1,0:T(8,128)(2,1)S(1)}, u32[]{:S(2)}) %copy-start) | copy-done | bytes 983064
  22.6 0.9 copy-done.2
  23.8 11.2 %collective-permute-done.1 = s32[384]{0:T(512)S(1)} collective-permute-done((s32[384]{0:T(512)S(1)}, s32[384]{0:T(512)S(1)}, u32[]{:S(2)}, u32[]{:S(2)}) %collective-permute-start.1) | collective-permute-done | bytes 1568 | tf_op jit(solution)/shard_map/ppermute | solution.py:21
  35.2 4.7 %collective-permute-start.4 = (bf16[2,5,384,128]{3,2,1,0:T(8,128)(2,1)}, bf16[2,5,384,128]{3,2,1,0:T(8,128)(2,1)}, u32[]{:S(2)}, u32[]{:S(2)}) collective-permute-start(bf16[2,5,384,128]{3,2,1,0:T(8,128)(2,1)} %collective-permute-done.2.ca), channel_id=1, source_target_pairs={{0,1},{1,2},{2,3},{3,4},{4,5},{5,6},{6,7},{8,9},{9,10},{10,11},{11... | collective-permute-start | bytes 2949128 | tf_op jit(solution)/shard_map/ppermute | solution.py:21
  40.0 1.9 %collective-permute-start.5 = (bf16[2,5,384,128]{3,2,1,0:T(8,128)(2,1)}, bf16[2,5,384,128]{3,2,1,0:T(8,128)(2,1)}, u32[]{:S(2)}, u32[]{:S(2)}) collective-permute-start(bf16[2,5,384,128]{3,2,1,0:T(8,128)(2,1)} %collective-permute-done.3.cb), channel_id=1, source_target_pairs={{0,1},{1,2},{2,3},{3,4},{4,5},{5,6},{6,7},{8,9},{9,10},{10,11},{11... | collective-permute-start | bytes 2949128 | tf_op jit(solution)/shard_map/ppermute | solution.py:21
  42.6 0.8 copy-done.4
  43.4 0.9 collective-permute-start.7
  44.6 6.7 %collective-permute-done.4.ea = bf16[2,5,384,128]{3,2,1,0:T(8,128)(2,1)} collective-permute-done((bf16[2,5,384,128]{3,2,1,0:T(8,128)(2,1)}, bf16[2,5,384,128]{3,2,1,0:T(8,128)(2,1)}, u32[]{:S(2)}, u32[]{:S(2)}) %collective-permute-start.4) | collective-permute-done | bytes 983072 | tf_op jit(solution)/shard_map/ppermute | solution.py:21
  51.3 10.5 %collective-permute-done.5.eb = bf16[2,5,384,128]{3,2,1,0:T(8,128)(2,1)} collective-permute-done((bf16[2,5,384,128]{3,2,1,0:T(8,128)(2,1)}, bf16[2,5,384,128]{3,2,1,0:T(8,128)(2,1)}, u32[]{:S(2)}, u32[]{:S(2)}) %collective-permute-start.5) | collective-permute-done | bytes 983072 | tf_op jit(solution)/shard_map/ppermute | solution.py:21
  61.8 1.0 %copy-done.5 = bf16[5,384,128]{2,1,0:T(8,128)(2,1)S(1)} copy-done((bf16[5,384,128]{2,1,0:T(8,128)(2,1)S(1)}, bf16[5,384,128]{2,1,0:T(8,128)(2,1)}, u32[]{:S(2)}) %copy-start.5) | copy-done | bytes 491544
  62.9 6.9 %attend.7 = (bf16[5,384,128]{2,1,0:T(8,128)(2,1)}, bf16[5,384,128]{2,1,0:T(8,128)(2,1)}) custom-call(bf16[5,384,128]{2,1,0:T(8,128)(2,1)S(1)} %collective-permute-done.10.qa, bf16[5,384,128]{2,1,0:T(8,128)(2,1)S(1)} %copy-done.5, bf16[2,5,384,128]{3,2,1,0:T(8,128)(2,1)} %collective-permute-done.2.ca, bf16[2,5,384,128]{3,2,1,0:T(8,128)(2,1)} %collective-permute-done.3.cb, ...), custom_call_target="tpu_custom_call" | custom-call | flops 1006632960 | bytes 5898240 | tf_op jit(solution)/shard_map/attend/pallas_call | solution.py:145
  70.0 1.2 %collective-permute-start.13 = (bf16[5,384,128]{2,1,0:T(8,128)(2,1)}, bf16[5,384,128]{2,1,0:T(8,128)(2,1)}, u32[]{:S(2)}, u32[]{:S(2)}) collective-permute-start(bf16[5,384,128]{2,1,0:T(8,128)(2,1)} %get-tuple-element.38), channel_id=1, source_target_pairs={{0,8},{8,0},{16,24},{24,16},{1,9},{9,1},{17,25},{25,17},{2,10},{10... | collective-permute-start | bytes 1474568 | tf_op jit(solution)/shard_map/ppermute | solution.py:188
  71.2 6.4 %attend.6 = (bf16[5,384,128]{2,1,0:T(8,128)(2,1)}, bf16[5,384,128]{2,1,0:T(8,128)(2,1)}) custom-call(bf16[5,384,128]{2,1,0:T(8,128)(2,1)S(1)} %collective-permute-done.6.qa, bf16[5,384,128]{2,1,0:T(8,128)(2,1)S(1)} %collective-permute-done.7.qb, bf16[2,10,384,128]{3,2,1,0:T(8,128)(2,1)S(1)} %get-tuple-element.23.ca.cb, ...), custom_call_target="tpu_custom_call" | custom-call | flops 1006632960 | bytes 5898240 | tf_op jit(solution)/shard_map/attend/pallas_call | solution.py:145
  77.5 1.2 %collective-permute-start.8 = (bf16[5,384,128]{2,1,0:T(8,128)(2,1)}, bf16[5,384,128]{2,1,0:T(8,128)(2,1)}, u32[]{:S(2)}, u32[]{:S(2)}) collective-permute-start(bf16[5,384,128]{2,1,0:T(8,128)(2,1)} %get-tuple-element.33), channel_id=1, source_target_pairs={{0,16},{16,0},{8,24},{24,8},{1,17},{17,1},{9,25},{25,9},{2,18},{18... | collective-permute-start | bytes 1474568 | tf_op jit(solution)/shard_map/ppermute | solution.py:188
  79.1 1.2 %copy-done.1 = bf16[10,384,128]{2,1,0:T(8,128)(2,1)S(1)} copy-done((bf16[10,384,128]{2,1,0:T(8,128)(2,1)S(1)}, bf16[10,384,128]{2,1,0:T(8,128)(2,1)}, u32[]{:S(2)}) %copy-start.1) | copy-done | bytes 983064
  80.3 6.2 %attend.5 = (bf16[5,384,128]{2,1,0:T(8,128)(2,1)S(1)}, bf16[5,384,128]{2,1,0:T(8,128)(2,1)S(1)}) custom-call(bf16[10,384,128]{2,1,0:T(8,128)(2,1)S(1)} %copy-done.1, bf16[10,384,128]{2,1,0:T(8,128)(2,1)S(1)} %copy-done.1, bf16[2,5,384,128]{3,2,1,0:T(8,128)(2,1)} %collective-permute-done.2.ca, bf16[2,5,384,128]{3,2,1,0:T(8,128)(2,1)} %collective-permute-done.3.cb, ...), custom_call_target="tpu_custom_call" | custom-call | flops 1006632960 | bytes 5898240 | tf_op jit(solution)/shard_map/attend/pallas_call | solution.py:145
  86.6 5.7 %attend.4 = (bf16[5,384,128]{2,1,0:T(8,128)(2,1)S(1)}, bf16[5,384,128]{2,1,0:T(8,128)(2,1)S(1)}) custom-call(bf16[10,384,128]{2,1,0:T(8,128)(2,1)S(1)} %copy-done.3, bf16[10,384,128]{2,1,0:T(8,128)(2,1)S(1)} %copy-done.3, bf16[2,10,384,128]{3,2,1,0:T(8,128)(2,1)S(1)} %get-tuple-element.23.ca.cb, bf16[2,10,384,128]{3,2,1,0:T(8,128)(2,1)S(1)} %get-tuple-element.23.ca.cb, ...), custom_call_target="tpu_custom_call" | custom-call | flops 1006632960 | bytes 5898240 | tf_op jit(solution)/shard_map/attend/pallas_call | solution.py:145
  92.3 5.3 %assemble.1 = bf16[384,40,128]{2,1,0:T(8,128)(2,1)} custom-call(s32[8]{0:T(128)S(1)} %stack.71.slots_ref, bf16[5,384,128]{2,1,0:T(8,128)(2,1)S(1)} %get-tuple-element.24.refs_0_, bf16[5,384,128]{2,1,0:T(8,128)(2,1)S(1)} %get-tuple-element.25.refs_1_, bf16[5,384,128]{2,1,0:T(8,128)(2,1)S(1)} %get-tuple-element.29.refs_2_, ...), custom_call_target="tpu_custom_call" | custom-call | tf_op jit(solution)/shard_map/assemble/pallas_call | solution.py:172
  (38 shorter events, 3.7 us)
Async XLA Ops:
  0.7 12.7 %copy-start.6 = (s32[384]{0:T(512)S(1)}, s32[384]{0:T(512)}, u32[]{:S(2)}) copy-start(s32[384]{0:T(512)} %param.7) | copy-start | bytes 4612
  5.8 29.4 %collective-permute-start.2 = (bf16[2,5,384,128]{3,2,1,0:T(8,128)(2,1)}, bf16[2,5,384,128]{3,2,1,0:T(8,128)(2,1)}, u32[]{:S(2)}, u32[]{:S(2)}) collective-permute-start(bf16[2,5,384,128]{3,2,1,0:T(8,128)(2,1)} %get-tuple-element.27), channel_id=1, source_target_pairs={{0,8},{8,0},{16,24},{24,16},{1,9},{9,1},{17,25},{25,17},{2,10},{10... | collective-permute-start | bytes 2949128 | tf_op jit(solution)/shard_map/ppermute | solution.py:188
  7.8 32.1 %collective-permute-start.3 = (bf16[2,5,384,128]{3,2,1,0:T(8,128)(2,1)}, bf16[2,5,384,128]{3,2,1,0:T(8,128)(2,1)}, u32[]{:S(2)}, u32[]{:S(2)}) collective-permute-start(bf16[2,5,384,128]{3,2,1,0:T(8,128)(2,1)} %get-tuple-element.28), channel_id=1, source_target_pairs={{0,16},{16,0},{8,24},{24,8},{1,17},{17,1},{9,25},{25,9},{2,18},{18... | collective-permute-start | bytes 2949128 | tf_op jit(solution)/shard_map/ppermute | solution.py:188
  9.1 62.1 %collective-permute-start = (bf16[2,10,384,128]{3,2,1,0:T(8,128)(2,1)S(1)}, bf16[2,10,384,128]{3,2,1,0:T(8,128)(2,1)}, u32[]{:S(2)}, u32[]{:S(2)}) collective-permute-start(bf16[2,10,384,128]{3,2,1,0:T(8,128)(2,1)S(1)} %get-tuple-element.23.ca.cb), channel_id=1, source_target_pairs={{0,1},{1,2},{2,3},{3,4},{4,5},{5,6},{6,7},{8,9},{9,10},{10,11},{11... | collective-permute-start | bytes 5898248 | tf_op jit(solution)/shard_map/ppermute | solution.py:21
  13.4 21.6 %collective-permute-start.1 = (s32[384]{0:T(512)S(1)}, s32[384]{0:T(512)S(1)}, u32[]{:S(2)}, u32[]{:S(2)}) collective-permute-start(s32[384]{0:T(512)S(1)} %copy-done.6), channel_id=1, source_target_pairs={{0,1},{1,2},{2,3},{3,4},{4,5},{5,6},{6,7},{8,9},{9,10},{10,11},{11... | collective-permute-start | bytes 4616 | tf_op jit(solution)/shard_map/ppermute | solution.py:21
  21.6 1.0 %copy-start = (bf16[10,384,128]{2,1,0:T(8,128)(2,1)}, bf16[10,384,128]{2,1,0:T(8,128)(2,1)S(1)}, u32[]{:S(2)}) copy-start(bf16[10,384,128]{2,1,0:T(8,128)(2,1)S(1)} %get-tuple-element.26.qa.qb) | copy-start | bytes 2949124
  22.6 0.9 copy-start.2
  23.5 18.5 %collective-permute-start.10 = (bf16[5,384,128]{2,1,0:T(8,128)(2,1)}, bf16[5,384,128]{2,1,0:T(8,128)(2,1)S(1)}, u32[]{:S(2)}, u32[]{:S(2)}) collective-permute-start(bf16[5,384,128]{2,1,0:T(8,128)(2,1)} %get-tuple-element.35), channel_id=1, source_target_pairs={{0,16},{16,0},{8,24},{24,8},{1,17},{17,1},{9,25},{25,9},{2,18},{18... | collective-permute-start | bytes 1474568 | tf_op jit(solution)/shard_map/ppermute | solution.py:188
  35.0 7.7 %collective-permute-start.11 = (bf16[5,384,128]{2,1,0:T(8,128)(2,1)S(1)}, bf16[5,384,128]{2,1,0:T(8,128)(2,1)S(1)}, u32[]{:S(2)}, u32[]{:S(2)}) collective-permute-start(bf16[5,384,128]{2,1,0:T(8,128)(2,1)S(1)} %get-tuple-element.36), channel_id=1, source_target_pairs={{0,8},{8,0},{16,24},{24,16},{1,9},{9,1},{17,25},{25,17},{2,10},{10... | collective-permute-start | bytes 1474568 | tf_op jit(solution)/shard_map/ppermute | solution.py:188
  35.2 16.1 %collective-permute-start.4 = (bf16[2,5,384,128]{3,2,1,0:T(8,128)(2,1)}, bf16[2,5,384,128]{3,2,1,0:T(8,128)(2,1)}, u32[]{:S(2)}, u32[]{:S(2)}) collective-permute-start(bf16[2,5,384,128]{3,2,1,0:T(8,128)(2,1)} %collective-permute-done.2.ca), channel_id=1, source_target_pairs={{0,1},{1,2},{2,3},{3,4},{4,5},{5,6},{6,7},{8,9},{9,10},{10,11},{11... | collective-permute-start | bytes 2949128 | tf_op jit(solution)/shard_map/ppermute | solution.py:21
  40.0 21.9 %collective-permute-start.5 = (bf16[2,5,384,128]{3,2,1,0:T(8,128)(2,1)}, bf16[2,5,384,128]{3,2,1,0:T(8,128)(2,1)}, u32[]{:S(2)}, u32[]{:S(2)}) collective-permute-start(bf16[2,5,384,128]{3,2,1,0:T(8,128)(2,1)} %collective-permute-done.3.cb), channel_id=1, source_target_pairs={{0,1},{1,2},{2,3},{3,4},{4,5},{5,6},{6,7},{8,9},{9,10},{10,11},{11... | collective-permute-start | bytes 2949128 | tf_op jit(solution)/shard_map/ppermute | solution.py:21
  42.1 29.1 %collective-permute-start.6 = (bf16[5,384,128]{2,1,0:T(8,128)(2,1)}, bf16[5,384,128]{2,1,0:T(8,128)(2,1)S(1)}, u32[]{:S(2)}, u32[]{:S(2)}) collective-permute-start(bf16[5,384,128]{2,1,0:T(8,128)(2,1)} %get-tuple-element.31), channel_id=1, source_target_pairs={{0,16},{16,0},{8,24},{24,8},{1,17},{17,1},{9,25},{25,9},{2,18},{18... | collective-permute-start | bytes 1474568 | tf_op jit(solution)/shard_map/ppermute | solution.py:188
  42.6 0.8 copy-start.4
  43.4 27.8 %collective-permute-start.7 = (bf16[5,384,128]{2,1,0:T(8,128)(2,1)}, bf16[5,384,128]{2,1,0:T(8,128)(2,1)S(1)}, u32[]{:S(2)}, u32[]{:S(2)}) collective-permute-start(bf16[5,384,128]{2,1,0:T(8,128)(2,1)} %get-tuple-element.32), channel_id=1, source_target_pairs={{0,8},{8,0},{16,24},{24,16},{1,9},{9,1},{17,25},{25,17},{2,10},{10... | collective-permute-start | bytes 1474568 | tf_op jit(solution)/shard_map/ppermute | solution.py:188
  61.8 1.0 %copy-start.5 = (bf16[5,384,128]{2,1,0:T(8,128)(2,1)S(1)}, bf16[5,384,128]{2,1,0:T(8,128)(2,1)}, u32[]{:S(2)}) copy-start(bf16[5,384,128]{2,1,0:T(8,128)(2,1)} %copy-done.4) | copy-start | bytes 1474564
  69.7 22.6 %collective-permute-start.12 = (bf16[5,384,128]{2,1,0:T(8,128)(2,1)}, bf16[5,384,128]{2,1,0:T(8,128)(2,1)S(1)}, u32[]{:S(2)}, u32[]{:S(2)}) collective-permute-start(bf16[5,384,128]{2,1,0:T(8,128)(2,1)} %get-tuple-element.37), channel_id=1, source_target_pairs={{0,16},{16,0},{8,24},{24,8},{1,17},{17,1},{9,25},{25,9},{2,18},{18... | collective-permute-start | bytes 1474568 | tf_op jit(solution)/shard_map/ppermute | solution.py:188
  70.0 22.4 %collective-permute-start.13 = (bf16[5,384,128]{2,1,0:T(8,128)(2,1)}, bf16[5,384,128]{2,1,0:T(8,128)(2,1)}, u32[]{:S(2)}, u32[]{:S(2)}) collective-permute-start(bf16[5,384,128]{2,1,0:T(8,128)(2,1)} %get-tuple-element.38), channel_id=1, source_target_pairs={{0,8},{8,0},{16,24},{24,16},{1,9},{9,1},{17,25},{25,17},{2,10},{10... | collective-permute-start | bytes 1474568 | tf_op jit(solution)/shard_map/ppermute | solution.py:188
  77.5 14.8 %collective-permute-start.8 = (bf16[5,384,128]{2,1,0:T(8,128)(2,1)}, bf16[5,384,128]{2,1,0:T(8,128)(2,1)}, u32[]{:S(2)}, u32[]{:S(2)}) collective-permute-start(bf16[5,384,128]{2,1,0:T(8,128)(2,1)} %get-tuple-element.33), channel_id=1, source_target_pairs={{0,16},{16,0},{8,24},{24,8},{1,17},{17,1},{9,25},{25,9},{2,18},{18... | collective-permute-start | bytes 1474568 | tf_op jit(solution)/shard_map/ppermute | solution.py:188
  78.8 13.6 %collective-permute-start.9 = (bf16[5,384,128]{2,1,0:T(8,128)(2,1)}, bf16[5,384,128]{2,1,0:T(8,128)(2,1)}, u32[]{:S(2)}, u32[]{:S(2)}) collective-permute-start(bf16[5,384,128]{2,1,0:T(8,128)(2,1)} %get-tuple-element.34), channel_id=1, source_target_pairs={{0,8},{8,0},{16,24},{24,16},{1,9},{9,1},{17,25},{25,17},{2,10},{10... | collective-permute-start | bytes 1474568 | tf_op jit(solution)/shard_map/ppermute | solution.py:188
  79.1 1.2 %copy-start.1 = (bf16[10,384,128]{2,1,0:T(8,128)(2,1)S(1)}, bf16[10,384,128]{2,1,0:T(8,128)(2,1)}, u32[]{:S(2)}) copy-start(bf16[10,384,128]{2,1,0:T(8,128)(2,1)} %copy-done) | copy-start | bytes 2949124
  80.3 6.2 %copy-start.3 = (bf16[10,384,128]{2,1,0:T(8,128)(2,1)S(1)}, bf16[10,384,128]{2,1,0:T(8,128)(2,1)}, u32[]{:S(2)}) copy-start(bf16[10,384,128]{2,1,0:T(8,128)(2,1)} %copy-done.2) | copy-start | bytes 2949124

commit v2 on v1

v2 whole, which is shorter than its diff:
```python
import functools

import jax
import jax.numpy as jnp
import numpy as np
from jax import lax
from jax.experimental import pallas as pl
from jax.experimental.pallas import tpu as pltpu
from jax.sharding import PartitionSpec as P

ACROSS_X = ((0, 1), (1, 0), (2, 3), (3, 2))
ACROSS_Y = ((0, 2), (2, 0), (1, 3), (3, 1))
BLOCK = 128
ROWS = 8
ID_BASE = 256
ID_ROWS = 16
PARAMS = pltpu.CompilerParams(vmem_limit_bytes=12 * 2**20)
IN_VMEM = pl.BlockSpec(memory_space=pltpu.VMEM)
IN_SMEM = pl.BlockSpec(memory_space=pltpu.SMEM)
NT = (((1,), (1,)), ((), ()))


def shifted(block, axis):
    size = lax.axis_size(axis)
    return lax.ppermute(block, axis, [(i, (i + 1) % size) for i in range(size)])


def turn(values, cosine, sine):
    return (values * cosine + pltpu.roll(values, values.shape[-1] // 2, 1) * sine).astype(jnp.bfloat16)


def prepare_cache(keys_values, positions, documents):
    tokens, _, heads, head_dim = keys_values.shape
    half = heads // 2
    half_dim = head_dim // 2
    steps = tokens // BLOCK
    chunk = BLOCK * heads * 2
    rows = jnp.transpose(keys_values, (0, 2, 1, 3)).reshape(tokens * heads * 2, head_dim)
    exponent = np.arange(half_dim, dtype=np.float32) * np.float32(2.0 / head_dim)
    inverse = np.power(np.float32(10000.0), -exponent).astype(np.float32)
    inverse = jnp.asarray(np.concatenate([inverse, inverse])[None])

    def kernel(positions_hbm, documents_hbm, inverse_hbm, rows_ref, all_ref, a_ref, b_ref, cosine_ref, sine_ref, *scratch):
        positions_ref, documents_ref, inverse_ref, ids, landed, wide, done, small_sems, row_sems, store_sems = scratch
        small = [
            pltpu.make_async_copy(positions_hbm, positions_ref, small_sems.at[0]),
            pltpu.make_async_copy(documents_hbm, documents_ref, small_sems.at[1]),
            pltpu.make_async_copy(inverse_hbm, inverse_ref, small_sems.at[2]),
        ]
        copies = [
            pltpu.make_async_copy(rows_ref.at[pl.ds(i * chunk, chunk)], landed.at[i], row_sems.at[i])
            for i in range(steps)
        ]
        for copy in (*small, *copies):
            copy.start()
        for copy in small:
            copy.wait()
        left = lax.broadcasted_iota(jnp.int32, (BLOCK, head_dim), 1) < half_dim
        columns = [
            jnp.transpose(jnp.broadcast_to(positions_ref[i : i + 1], (BLOCK, BLOCK))).astype(jnp.float32)
            for i in range(steps)
        ]
        for i in range(0, steps, 2):
            other = min(i + 1, steps - 1)
            angles = jnp.where(left, columns[i], columns[other]) * inverse_ref[...]
            cosine, sine = jnp.cos(angles), jnp.sin(angles)
            turned_cosine, turned_sine = (pltpu.roll(t, half_dim, 1) for t in (cosine, sine))
            for k, (c, s) in enumerate(
                (
                    (jnp.where(left, cosine, turned_cosine), jnp.where(left, -sine, turned_sine)),
                    (jnp.where(left, turned_cosine, cosine), jnp.where(left, -turned_sine, sine)),
                )
            ):
                if i + k < steps:
                    at = slice((i + k) * BLOCK, (i + k + 1) * BLOCK)
                    cosine_ref[at] = c
                    sine_ref[at] = s
        ids[...] = jnp.concatenate(
            [
                documents_ref[...] // ID_BASE,
                documents_ref[...] % ID_BASE,
                jnp.zeros((ID_ROWS - 2 * steps, BLOCK), jnp.int32),
            ],
            axis=0,
        ).astype(jnp.float32).astype(jnp.bfloat16)
        stores = [
            pltpu.make_async_copy(ids, all_ref.at[2 * heads, pl.ds(0, ID_ROWS)], store_sems.at[0])
        ]
        stores[0].start()
        for i in range(steps):
            at = slice(i * BLOCK, (i + 1) * BLOCK)
            copies[i].wait()
            wide[...] = landed[i].astype(jnp.float32)
            for head in range(heads):
                key = wide[pl.ds(2 * head, BLOCK, stride=2 * heads), :]
                done[i, head] = turn(key, cosine_ref[at], sine_ref[at])
                done[i, heads + head] = wide[pl.ds(2 * head + 1, BLOCK, stride=2 * heads), :].astype(jnp.bfloat16)
            rows_at = pl.ds(i * BLOCK, BLOCK)
            moves = [(done.at[i], all_ref.at[pl.ds(0, 2 * heads), rows_at])]
            for k in range(2):
                moves.append((done.at[i, pl.ds(k * heads, half)], a_ref.at[k, :, rows_at]))
                moves.append((done.at[i, pl.ds(k * heads + half, heads - half)], b_ref.at[k, :, rows_at]))
            for source, target in moves:
                store = pltpu.make_async_copy(source, target, store_sems.at[len(stores)])
                store.start()
                stores.append(store)
        for store in stores:
            store.wait()

    table = jax.ShapeDtypeStruct((tokens, head_dim), jnp.float32)
    anywhere = pl.BlockSpec(memory_space=pl.ANY)
    return pl.pallas_call(
        kernel,
        in_specs=[anywhere] * 4,
        out_specs=[anywhere] * 3 + [IN_VMEM] * 2,
        out_shape=[
            jax.ShapeDtypeStruct((2 * heads + 1, tokens, head_dim), jnp.bfloat16),
            *(jax.ShapeDtypeStruct((2, n, tokens, head_dim), jnp.bfloat16) for n in (half, heads - half)),
            table,
            table,
        ],
        scratch_shapes=[
            pltpu.VMEM((steps, BLOCK), jnp.int32),
            pltpu.VMEM((steps, BLOCK), jnp.int32),
            pltpu.VMEM((1, head_dim), jnp.float32),
            pltpu.VMEM((ID_ROWS, BLOCK), jnp.bfloat16),
            pltpu.VMEM((steps, chunk, head_dim), jnp.bfloat16),
            pltpu.VMEM((chunk, head_dim), jnp.float32),
            pltpu.VMEM((steps, 2 * heads, BLOCK, head_dim), jnp.bfloat16),
            pltpu.SemaphoreType.DMA((3,)),
            pltpu.SemaphoreType.DMA((steps,)),
            pltpu.SemaphoreType.DMA((1 + 5 * steps,)),
        ],
        compiler_params=pltpu.CompilerParams(vmem_limit_bytes=60 * 2**20),
        name="prepare_cache",
    )(positions.reshape(steps, BLOCK), documents.reshape(steps, BLOCK), inverse, rows)


def prepare_queries(queries, cosine, sine, starts, counts):
    tokens, heads, head_dim = queries.shape

    def kernel(starts_ref, queries_ref, cosine_ref, sine_ref, *refs):
        wide = refs[-1]
        wide[...] = queries_ref[...].reshape(tokens * heads, head_dim).astype(jnp.float32)
        run = 0
        for out_ref, runs in zip(refs[:-1], counts):
            slot = 0
            for count in runs:
                for i in range(count):
                    head = wide[pl.ds(starts_ref[run] + i, tokens, stride=heads), :]
                    out_ref[slot] = turn(head, cosine_ref[...], sine_ref[...])
                    slot += 1
                run += 1

    totals = [sum(runs) for runs in counts]
    return pl.pallas_call(
        kernel,
        in_specs=[IN_SMEM] + [IN_VMEM] * 3,
        out_specs=[IN_VMEM] * len(totals),
        out_shape=[jax.ShapeDtypeStruct((n, tokens, head_dim), jnp.bfloat16) for n in totals],
        scratch_shapes=[pltpu.VMEM((tokens * heads, head_dim), jnp.float32)],
        compiler_params=PARAMS,
        cost_estimate=pl.CostEstimate(
            flops=2 * 10**9, bytes_accessed=4 * queries.size, transcendentals=0
        ),
        name="prepare_queries",
    )(starts, queries, cosine, sine)


def attend(sets, documents, earlier_docs, flops=1):
    count = sets[0][0][2]
    tokens, head_dim = sets[0][0][0].shape[-2:]
    blocks = tokens // BLOCK
    width = tokens + BLOCK
    scale = float(head_dim**-0.5 * np.log2(np.e))
    n = len(sets)

    def kernel(docs_ref, earlier_ref, *refs):
        bias = refs[-1]
        window = [earlier_ref[i : i + 1] for i in range(blocks)] + [docs_ref[i : i + 1] for i in range(blocks)]
        row = lax.broadcasted_iota(jnp.int32, (BLOCK, BLOCK), 0)
        column = lax.broadcasted_iota(jnp.int32, (BLOCK, BLOCK), 1)
        for r in range(blocks):
            mine = jnp.transpose(jnp.broadcast_to(docs_ref[r : r + 1], (BLOCK, BLOCK)))
            for c in range(blocks + 1):
                allowed = window[r + c] == mine
                if c == blocks:
                    allowed = jnp.logical_and(allowed, column <= row)
                bias[r, :, c * BLOCK : (c + 1) * BLOCK] = jnp.where(allowed, 0.0, -1e30)
        for head in range(count):
            for g, group in enumerate(sets):
                q, c, e = refs[3 * g : 3 * g + 3]
                q_head = group[0][1] + head

                def band(kind, low, high):
                    (_, c_first, c_heads), (_, e_first, e_heads) = group[1:]
                    c_row = (kind * c_heads + c_first + head) * tokens
                    e_row = (kind * e_heads + e_first + head) * tokens
                    return jnp.concatenate([e[e_row + low : e_row + tokens], c[c_row : c_row + high]], axis=0)

                for r in range(blocks):
                    low, high = BLOCK * r, BLOCK * (r + 1)
                    key, value = band(0, low, high), band(1, low, high)
                    scores = lax.dot_general(q[q_head, low:high], key, NT, preferred_element_type=jnp.float32)
                    scores = scores + bias[r]
                    largest = jnp.max(scores, axis=1, keepdims=True) * scale
                    weights = jnp.exp2(scores * scale - largest).astype(jnp.bfloat16)
                    extended = jnp.concatenate([value, jnp.ones_like(value)], axis=1)
                    mixed = jnp.dot(weights, extended, preferred_element_type=jnp.float32)
                    mixed = (mixed[:, :head_dim] / mixed[:, head_dim:]).astype(jnp.bfloat16)
                    refs[3 * n + g][head, low:high] = mixed

    return pl.pallas_call(
        kernel,
        in_specs=[IN_VMEM] * (2 + 3 * n),
        out_specs=[IN_VMEM] * n,
        out_shape=[jax.ShapeDtypeStruct((count, tokens, head_dim), jnp.bfloat16)] * n,
        scratch_shapes=[pltpu.VMEM((blocks, BLOCK, width), jnp.float32)],
        compiler_params=PARAMS,
        cost_estimate=pl.CostEstimate(flops=flops, bytes_accessed=1, transcendentals=0),
        name="attend",
    )(documents.reshape(blocks, BLOCK), earlier_docs.reshape(blocks, BLOCK), *[o[0] for group in sets for o in group])


def assemble(pieces, slots, heads, window_start=None, window=0):
    count, tokens, head_dim = pieces[0].shape
    step = BLOCK

    def kernel(slots_ref, *refs):
        piece_refs, outs, gathered = refs[: len(pieces)], refs[len(pieces) : -1], refs[-1]
        for p, ref in enumerate(piece_refs):
            gathered[pl.ds(slots_ref[p] * count, count)] = ref[...]
        outs[0][...] = jnp.swapaxes(gathered[...], 0, 1)
        if window:
            first = pl.multiple_of(slots_ref[len(pieces)] * ROWS, ROWS)
            outs[1][...] = jnp.swapaxes(gathered[pl.ds(first, window)], 0, 1)

    if window:
        slots = jnp.concatenate([slots, window_start[None]])
    counts = (heads, window) if window else (heads,)
    return pl.pallas_call(
        kernel,
        grid_spec=pltpu.PrefetchScalarGridSpec(
            num_scalar_prefetch=1,
            grid=(tokens // step,),
            in_specs=[pl.BlockSpec((count, step, head_dim), lambda i, s: (0, i, 0))] * len(pieces),
            out_specs=[pl.BlockSpec((step, n, head_dim), lambda i, s: (i, 0, 0)) for n in counts],
            scratch_shapes=[pltpu.VMEM((heads, step, head_dim), jnp.bfloat16)],
        ),
        out_shape=[jax.ShapeDtypeStruct((tokens, n, head_dim), jnp.bfloat16) for n in counts],
        compiler_params=PARAMS,
        cost_estimate=pl.CostEstimate(flops=10**9, bytes_accessed=1, transcendentals=0),
        name="assemble",
    )(slots, *pieces)


def complete(gathered, old, pieces, slot):
    count, tokens, head_dim = pieces[0].shape
    mine = 2 * count
    window = old.shape[1]

    def kernel(slot_ref, first_ref, second_ref, old_ref, _, out_ref, placed):
        j = pl.program_id(0)
        block = (slot_ref[0] * mine) // ROWS
        low = slot_ref[0] * mine - block * ROWS

        @pl.when(j == 0)
        def _():
            placed[pl.ds(low, count)] = first_ref[...]
            placed[pl.ds(low + count, count)] = second_ref[...]

        row = lax.broadcasted_iota(jnp.int32, (tokens, ROWS, head_dim), 1) + j * ROWS
        new = jnp.swapaxes(placed[pl.ds(pl.multiple_of(j * ROWS, ROWS), ROWS)], 0, 1)
        keep = jnp.logical_or(row < low, row >= low + mine)
        out_ref[...] = jnp.where(keep, old_ref[...], new)

    piece = pl.BlockSpec((count, tokens, head_dim), lambda j, s: (0, 0, 0))
    return pl.pallas_call(
        kernel,
        grid_spec=pltpu.PrefetchScalarGridSpec(
            num_scalar_prefetch=1,
            grid=(window // ROWS,),
            in_specs=[
                piece,
                piece,
                pl.BlockSpec((tokens, ROWS, head_dim), lambda j, s: (0, j, 0)),
                pl.BlockSpec(memory_space=pl.ANY),
            ],
            out_specs=pl.BlockSpec((tokens, ROWS, head_dim), lambda j, s: (0, (s[0] * mine) // ROWS + j, 0)),
            scratch_shapes=[pltpu.VMEM((window, tokens, head_dim), jnp.bfloat16)],
        ),
        out_shape=jax.ShapeDtypeStruct(gathered.shape, gathered.dtype),
        input_output_aliases={4: 0},
        compiler_params=PARAMS,
        name="complete",
    )(slot, *pieces, old, gathered)


def across(value, route):
    return lax.ppermute(value, "section", route)


def rows_of(array):
    return array.reshape(-1, array.shape[-1])


def after(values, others):
    return lax.optimization_barrier((values, others))[0]


def square_body(queries, keys_values, positions, documents):
    mine = keys_values.shape[2]
    half = mine // 2
    section = lax.axis_index("section")
    beside_x, beside_y, opposite = section ^ 1, section ^ 2, section ^ 3
    tokens = documents.shape[0]
    share, share_a, share_b, cosine, sine = prepare_cache(keys_values, positions, documents)
    cache_a = across(share_a, ACROSS_X)
    cache_b = across(share_b, ACROSS_Y)
    before = shifted(share, "ctx")

    starts = jnp.stack(
        [
            beside_y * mine,
            beside_x * mine + half,
            opposite * mine,
            opposite * mine + half,
            section * mine,
            beside_x * mine,
            beside_y * mine + half,
        ]
    ).astype(jnp.int32)
    near_y, near_x, far_y, far_x, own_near, own_far = prepare_queries(
        queries[0], cosine, sine, starts, ((half,), (half,), (half,), (half,), (mine,), (half, half))
    )
    near_a = across(near_y, ACROSS_Y)
    near_b = across(near_x, ACROSS_X)
    cache_a, cache_b = after((cache_a, cache_b), (near_y, before))
    earlier_a = shifted(cache_a, "ctx")
    earlier_b = shifted(cache_b, "ctx")
    far_a = across(far_y, ACROSS_Y)
    far_b = across(far_x, ACROSS_X)

    blocks = tokens // BLOCK
    ids = before[2 * mine].astype(jnp.int32)
    share, before = rows_of(share), rows_of(before)
    earlier_docs = ids[:blocks] * ID_BASE + ids[blocks : 2 * blocks]
    earlier_docs = jnp.where(lax.axis_index("ctx") == 0, -1, earlier_docs)
    near = (((share, 0, mine), (before, 0, mine)), ((share, half, mine), (before, half, mine)))
    out_near_a, out_near_b = attend(
        (((near_a, 0, half), *near[0]), ((near_b, 0, half), *near[1])), documents, earlier_docs, 5 * 10**10
    )
    back_near_a = across(out_near_a, ACROSS_Y)
    back_near_b = across(after(out_near_b, earlier_a), ACROSS_X)
    own_near = after(own_near, out_near_a)
    own_near_a, own_near_b = attend(
        (((own_near, 0, half), *near[0]), ((own_near, half, half), *near[1])), documents, earlier_docs
    )
    far_a, earlier_a = after((far_a, earlier_a), own_near_a)
    far_of_a = tuple((rows_of(c), 0, half) for c in (cache_a, earlier_a))
    (out_far_a,) = attend((((far_a, 0, half), *far_of_a),), documents, earlier_docs)
    back_far_a = across(out_far_a, ACROSS_Y)
    far_b, earlier_b = after((far_b, earlier_b), out_far_a)
    far_of_b = tuple((rows_of(c), 0, half) for c in (cache_b, earlier_b))
    (out_far_b,) = attend((((far_b, 0, half), *far_of_b),), documents, earlier_docs)
    back_far_b = across(out_far_b, ACROSS_X)
    own_far = after(own_far, out_far_b)
    own_far_a, own_far_b = attend(
        (((own_far, 0, half), *far_of_a), ((own_far, half, half), *far_of_b)), documents, earlier_docs
    )

    slots = jnp.stack(
        [2 * section, 2 * section + 1, 2 * beside_x, 2 * beside_y + 1, 2 * beside_y, 2 * beside_x + 1]
    ).astype(jnp.int32)
    pieces = (own_near_a, own_near_b, own_far_a, own_far_b, back_near_a, back_near_b)
    start = (opposite * mine) // ROWS
    window = -(-mine // ROWS) * ROWS
    gathered, old = assemble(pieces, slots, queries.shape[2], start.astype(jnp.int32), window)
    back_far_a = after(back_far_a, gathered)
    back_far_b = after(back_far_b, back_far_a)
    return complete(gathered, old, (back_far_a, back_far_b), opposite[None].astype(jnp.int32))[None]


def general_body(queries, keys_values, positions, documents):
    heads = queries.shape[2]
    mine = keys_values.shape[2]
    earlier_docs = shifted(documents, "ctx")
    earlier_docs = jnp.where(lax.axis_index("ctx") == 0, -1, earlier_docs)
    share, _, _, cosine, sine = prepare_cache(keys_values, positions, documents)
    share = share[:-1].reshape(2, mine, *share.shape[1:])
    whole = lax.all_gather(share, "section", axis=1, tiled=True)
    earlier = shifted(whole, "ctx")
    starts = jnp.zeros((1,), jnp.int32)
    (rotated,) = prepare_queries(queries[0], cosine, sine, starts, ((heads,),))
    outs = []
    for first in range(0, heads, mine):
        chunk = slice(first, first + mine)
        caches = ((rows_of(c[:, chunk]), 0, mine) for c in (whole, earlier))
        group = ((rotated[chunk], 0, mine), *caches)
        outs += attend((group,), documents, earlier_docs)
    return assemble(outs, jnp.arange(len(outs), dtype=jnp.int32), heads)[0][None]


def solution(mesh):
    placed = (P("section", "ctx", None, None), P("ctx", None, "section", None), P("ctx"), P("ctx"))
    body = square_body if mesh.shape["section"] == 4 else general_body
    return jax.shard_map(
        body, mesh=mesh, in_specs=placed, out_specs=P("section", "ctx", None, None), check_vma=False
    )
```

time: 99.4 us -> 78.7 us (0.79)
  starting transfers between devices: 20.8 us -> 12.2 us
  waiting for transfers between devices: 28.8 us -> 20.6 us
  Pallas kernels: 40.8 us -> 34.9 us
  local copies, waits for them, and re-layouts: 5.12 us -> 9.61 us
  other arithmetic: 1.96 us -> 0.03 us
    ppermute x4 -> x3, waiting for transfers between devices: 28.5 us -> 0.01 us  [shifted(): return lax.ppermute(block, axis, [(i, (i + 1) % size) for i in range(size)])]
    ppermute x10, waiting for transfers between devices: 0.31 us -> 20.6 us  [across(): return lax.ppermute(value, 'section', route)]
    ppermute x4 -> x3, starting transfers between devices: 12.9 us -> 3.9 us  [shifted(): return lax.ppermute(block, axis, [(i, (i + 1) % size) for i in range(size)])]
    pallas_call x6 -> x8, Pallas kernels: 35.5 us -> 29.9 us  [the longest x5 17 us: attend(): pl.pallas_call(kernel, in_specs=[IN_VMEM] * (2 + 3 * n), out_specs=[IN_VM...]
    unnamed x14 -> x30, local copies, waits for them, and re-layouts: 4.94 us -> 9.45 us
  transfers between devices with their start and end apart: 14 -> 13, of which waited for: 4 -> 4; matrix products, arithmetic and copies ran while one was open for 1% -> 0% of each run, Pallas kernels for 32% -> 35%
where the time goes in v2:
time: 78.7 us; the launch traced here: 77.5 us
  Pallas kernels  34.9 us (44%)
  waiting for transfers between devices  20.6 us (26%)
  starting transfers between devices  12.2 us (16%)
  local copies, waits for them, and re-layouts  9.61 us (12%)
    ppermute x10, waiting for transfers between devices, across(): return lax.ppermute(value, 'section', route)  20.6 us
    pallas_call x5, Pallas kernels, attend(): pl.pallas_call(kernel, in_specs=[IN_VMEM] * (2 + 3 * n), out_specs=[IN_VM...  17 us
    unnamed x30, local copies, waits for them, and re-layouts  9.45 us
    ppermute x10, starting transfers between devices, across(): return lax.ppermute(value, 'section', route)  8.3 us
    pallas_call x1, Pallas kernels, prepare_queries(): pl.pallas_call(kernel, in_specs=[IN_SMEM] + [IN_VMEM] * 3, out_specs=[IN_...  5.23 us
    pallas_call x1, Pallas kernels, assemble(): pl.pallas_call(kernel, grid_spec=pltpu.PrefetchScalarGridSpec(num_scalar_...  4.93 us
    pallas_call x1, Pallas kernels, prepare_cache(): pl.pallas_call(kernel, in_specs=[anywhere] * 4, out_specs=[anywhere] * 3...  4.9 us
    ppermute x3, starting transfers between devices, shifted(): return lax.ppermute(block, axis, [(i, (i + 1) % size) for i in range(size)])  3.9 us
  transfers between devices with their start and end apart: 13, of which 4 were waited for; matrix products, arithmetic and copies ran while one was open for 0% of the time, Pallas kernels for 35%

profile of v2, /device:TPU:1, one launch (start us, length us, event | category | flops | bytes accessed | tf_op | source)
XLA Modules:
  0.0 77.5 jit_solution(14811420350087253338)
XLA Ops:
  0.0 4.9 %prepare_cache.1 = (bf16[21,384,128]{2,1,0:T(8,128)(2,1)}, bf16[2,5,384,128]{3,2,1,0:T(8,128)(2,1)}, bf16[2,5,384,128]{3,2,1,0:T(8,128)(2,1)}, f32[384,128]{1,0:T(8,128)}, f32[384,128]{1,0:T(8,128)}) custom-call(s32[3,128]{1,0:T(4,128)} %bitcast.50, s32[3,128]{1,0:T(4,128)} %bitcast.42, f32[1,128]{1,0:T(1,128)} %constant.38.clone.inverse_hbm, ...), custom_call_target="tpu_custom_call" | custom-call | tf_op jit(solution)/shard_map/prepare_cache/pallas_call | solution.py:112
  4.9 2.7 %collective-permute-start = (bf16[21,384,128]{2,1,0:T(8,128)(2,1)}, bf16[21,384,128]{2,1,0:T(8,128)(2,1)S(1)}, u32[]{:S(2)}, u32[]{:S(2)}) collective-permute-start(bf16[21,384,128]{2,1,0:T(8,128)(2,1)} %get-tuple-element.35), channel_id=1, source_target_pairs={{0,1},{1,2},{2,3},{3,4},{4,5},{5,6},{6,7},{7,0},{8,9},{9,10},{10,1... | collective-permute-start | bytes 6193160 | tf_op jit(solution)/shard_map/ppermute | solution.py:25
  7.6 1.2 %collective-permute-start.2 = (bf16[2,5,384,128]{3,2,1,0:T(8,128)(2,1)}, bf16[2,5,384,128]{3,2,1,0:T(8,128)(2,1)}, u32[]{:S(2)}, u32[]{:S(2)}) collective-permute-start(bf16[2,5,384,128]{3,2,1,0:T(8,128)(2,1)} %get-tuple-element.39), channel_id=1, source_target_pairs={{0,8},{8,0},{16,24},{24,16},{1,9},{9,1},{17,25},{25,17},{2,10},{10... | collective-permute-start | bytes 2949128 | tf_op jit(solution)/shard_map/ppermute | solution.py:300
  8.9 1.2 %collective-permute-start.3 = (bf16[2,5,384,128]{3,2,1,0:T(8,128)(2,1)}, bf16[2,5,384,128]{3,2,1,0:T(8,128)(2,1)}, u32[]{:S(2)}, u32[]{:S(2)}) collective-permute-start(bf16[2,5,384,128]{3,2,1,0:T(8,128)(2,1)} %get-tuple-element.40), channel_id=1, source_target_pairs={{0,16},{16,0},{8,24},{24,8},{1,17},{17,1},{9,25},{25,9},{2,18},{18... | collective-permute-start | bytes 2949128 | tf_op jit(solution)/shard_map/ppermute | solution.py:300
  10.2 2.1 %copy-done.8 = bf16[1,384,40,128]{3,2,1,0:T(8,128)(2,1)S(1)} copy-done((bf16[1,384,40,128]{3,2,1,0:T(8,128)(2,1)S(1)}, bf16[1,384,40,128]{3,2,1,0:T(8,128)(2,1)}, u32[]{:S(2)}) %copy-start.8) | copy-done | bytes 3932184
  14.2 5.2 %prepare_queries.1 = (bf16[5,384,128]{2,1,0:T(8,128)(2,1)}, bf16[5,384,128]{2,1,0:T(8,128)(2,1)}, bf16[5,384,128]{2,1,0:T(8,128)(2,1)}, bf16[5,384,128]{2,1,0:T(...) custom-call(s32[7]{0:T(128)S(1)} %stack.49.starts_ref, ...), custom_call_target="tpu_custom_call" | custom-call | flops 2000000000 | bytes 7864320 | tf_op jit(solution)/shard_map/prepare_queries/pallas_call | solution.py:156
  19.4 0.9 %copy-done.5 = bf16[10,384,128]{2,1,0:T(8,128)(2,1)} copy-done((bf16[10,384,128]{2,1,0:T(8,128)(2,1)}, bf16[10,384,128]{2,1,0:T(8,128)(2,1)S(1)}, u32[]{:S(2)}) %copy-start.5) | copy-done | bytes 983064
  20.8 10.9 %collective-permute-done.2 = bf16[2,5,384,128]{3,2,1,0:T(8,128)(2,1)} collective-permute-done((bf16[2,5,384,128]{3,2,1,0:T(8,128)(2,1)}, bf16[2,5,384,128]{3,2,1,0:T(8,128)(2,1)}, u32[]{:S(2)}, u32[]{:S(2)}) %collective-permute-start.2) | collective-permute-done | bytes 983072 | tf_op jit(solution)/shard_map/ppermute | solution.py:300
  31.8 1.2 %collective-permute-start.1 = (bf16[5,384,128]{2,1,0:T(8,128)(2,1)}, bf16[5,384,128]{2,1,0:T(8,128)(2,1)S(1)}, u32[]{:S(2)}, u32[]{:S(2)}) collective-permute-start(bf16[5,384,128]{2,1,0:T(8,128)(2,1)} %get-tuple-element.38), channel_id=1, source_target_pairs={{0,16},{16,0},{8,24},{24,8},{1,17},{17,1},{9,25},{25,9},{2,18},{18... | collective-permute-start | bytes 1474568 | tf_op jit(solution)/shard_map/ppermute | solution.py:300
  32.9 1.2 %collective-permute-start.8 = (bf16[5,384,128]{2,1,0:T(8,128)(2,1)}, bf16[5,384,128]{2,1,0:T(8,128)(2,1)S(1)}, u32[]{:S(2)}, u32[]{:S(2)}) collective-permute-start(bf16[5,384,128]{2,1,0:T(8,128)(2,1)} %get-tuple-element.52), channel_id=1, source_target_pairs={{0,8},{8,0},{16,24},{24,16},{1,9},{9,1},{17,25},{25,17},{2,10},{10... | collective-permute-start | bytes 1474568 | tf_op jit(solution)/shard_map/ppermute | solution.py:300
  34.1 1.0 %collective-permute-start.4 = (bf16[2,5,384,128]{3,2,1,0:T(8,128)(2,1)}, bf16[2,5,384,128]{3,2,1,0:T(8,128)(2,1)S(1)}, u32[]{:S(2)}, u32[]{:S(2)}) collective-permute-start(bf16[2,5,384,128]{3,2,1,0:T(8,128)(2,1)} %collective-permute-done.2), channel_id=1, source_target_pairs={{0,1},{1,2},{2,3},{3,4},{4,5},{5,6},{6,7},{7,0},{8,9},{9,10},{10,1... | collective-permute-start | bytes 2949128 | tf_op jit(solution)/shard_map/ppermute | solution.py:25
  35.1 7.2 %collective-permute-done.6.refs_3_ = bf16[5,384,128]{2,1,0:T(8,128)(2,1)S(1)} collective-permute-done((bf16[5,384,128]{2,1,0:T(8,128)(2,1)}, bf16[5,384,128]{2,1,0:T(8,128)(2,1)S(1)}, u32[]{:S(2)}, u32[]{:S(2)}) %collective-permute-start.6) | collective-permute-done | bytes 491552 | tf_op jit(solution)/shard_map/ppermute | solution.py:300
  43.3 1.6 %copy-done = bf16[21,384,128]{2,1,0:T(8,128)(2,1)S(1)} copy-done((bf16[21,384,128]{2,1,0:T(8,128)(2,1)S(1)}, bf16[21,384,128]{2,1,0:T(8,128)(2,1)}, u32[]{:S(2)}) %copy-start) | copy-done | bytes 2064408
  44.9 4.5 %attend.5 = (bf16[5,384,128]{2,1,0:T(8,128)(2,1)}, bf16[5,384,128]{2,1,0:T(8,128)(2,1)}) custom-call(s32[3,128]{1,0:T(4,128)S(1)} %bitcast.43, s32[3,128]{1,0:T(4,128)S(1)} %fusion.1.earlier_ref, bf16[5,384,128]{2,1,0:T(8,128)(2,1)} %collective-permute-done.5.refs_0_, bf16[8064,128]{1,0:T(8,128)(2,1)S(1)} %bitcast.34, bf16[8064,128]{1,0:T(8,128)(2,1)S(1)} %bitcast.30, ...), custom_call_target="tpu_custom_call" | custom-call | flops 49999998976 | bytes 1 | tf_op jit(solution)/shard_map/attend/pallas_call | solution.py:213
  49.4 1.2 %collective-permute-start.10 = (bf16[5,384,128]{2,1,0:T(8,128)(2,1)}, bf16[5,384,128]{2,1,0:T(8,128)(2,1)}, u32[]{:S(2)}, u32[]{:S(2)}) collective-permute-start(bf16[5,384,128]{2,1,0:T(8,128)(2,1)} %get-tuple-element.45), channel_id=1, source_target_pairs={{0,16},{16,0},{8,24},{24,8},{1,17},{17,1},{9,25},{25,9},{2,18},{18... | collective-permute-start | bytes 1474568 | tf_op jit(solution)/shard_map/ppermute | solution.py:300
  51.1 2.7 %attend.6 = (bf16[5,384,128]{2,1,0:T(8,128)(2,1)S(1)}, bf16[5,384,128]{2,1,0:T(8,128)(2,1)S(1)}) custom-call(s32[3,128]{1,0:T(4,128)S(1)} %bitcast.44, s32[3,128]{1,0:T(4,128)S(1)} %fusion.1.earlier_ref, bf16[10,384,128]{2,1,0:T(8,128)(2,1)S(1)} %copy-done.6, bf16[8064,128]{1,0:T(8,128)(2,1)S(1)} %bitcast.36, bf16[8064,128]{1,0:T(8,128)(2,1)S(1)} %bitcast.32, ...), custom_call_target="tpu_custom_call" | custom-call | flops 1 | bytes 1 | tf_op jit(solution)/shard_map/attend/pallas_call | solution.py:213
  54.5 2.9 %attend.7 = bf16[5,384,128]{2,1,0:T(8,128)(2,1)S(1)} custom-call(s32[3,128]{1,0:T(4,128)S(1)} %bitcast.45, s32[3,128]{1,0:T(4,128)S(1)} %fusion.1.earlier_ref, bf16[5,384,128]{2,1,0:T(8,128)(2,1)S(1)} %collective-permute-done.1.refs_0_, bf16[3840,128]{1,0:T(8,128)(2,1)} %bitcast.16.refs_1_, bf16[3840,128]{1,0:T(8,128)(2,1)S(1)} %bitcast.38), custom_call_target="tpu_custom_call" | custom-call | flops 1 | bytes 1 | tf_op jit(solution)/shard_map/attend/pallas_call | solution.py:213
  58.0 2.8 %attend.8 = bf16[5,384,128]{2,1,0:T(8,128)(2,1)S(1)} custom-call(s32[3,128]{1,0:T(4,128)S(1)} %bitcast.46, s32[3,128]{1,0:T(4,128)S(1)} %fusion.1.earlier_ref, bf16[5,384,128]{2,1,0:T(8,128)(2,1)S(1)} %collective-permute-done.8.refs_0_, bf16[3840,128]{1,0:T(8,128)(2,1)} %bitcast.25.refs_1_.refs_4_, bf16[3840,128]{1,0:T(8,128)(2,1)S(1)} %bitcast.40), custom_call_target="tpu_custom_call" | custom-call | flops 1 | bytes 1 | tf_op jit(solution)/shard_map/attend/pallas_call | solution.py:213
  60.8 0.9 %copy-done.3 = bf16[2,5,384,128]{3,2,1,0:T(8,128)(2,1)} copy-done((bf16[2,5,384,128]{3,2,1,0:T(8,128)(2,1)}, bf16[2,5,384,128]{3,2,1,0:T(8,128)(2,1)S(1)}, u32[]{:S(2)}) %copy-start.3) | copy-done | bytes 983064
  62.6 1.2 %copy-done.4 = bf16[2,5,384,128]{3,2,1,0:T(8,128)(2,1)S(1)} copy-done((bf16[2,5,384,128]{3,2,1,0:T(8,128)(2,1)S(1)}, bf16[2,5,384,128]{3,2,1,0:T(8,128)(2,1)}, u32[]{:S(2)}) %copy-start.4) | copy-done | bytes 983064
  63.8 4.2 %attend.9 = (bf16[5,384,128]{2,1,0:T(8,128)(2,1)S(1)}, bf16[5,384,128]{2,1,0:T(8,128)(2,1)S(1)}) custom-call(s32[3,128]{1,0:T(4,128)S(1)} %bitcast.47, s32[3,128]{1,0:T(4,128)S(1)} %fusion.1.earlier_ref, bf16[10,384,128]{2,1,0:T(8,128)(2,1)S(1)} %get-tuple-element.56.refs_0_.refs_3_, bf16[3840,128]{1,0:T(8,128)(2,1)} %bitcast.16.refs_1_, ...), custom_call_target="tpu_custom_call" | custom-call | flops 1 | bytes 1 | tf_op jit(solution)/shard_map/attend/pallas_call | solution.py:213
  68.1 4.9 %assemble.1 = (bf16[384,40,128]{2,1,0:T(8,128)(2,1)}, bf16[384,16,128]{2,1,0:T(8,128)(2,1)S(1)}) custom-call(s32[7]{0:T(128)S(1)} %concatenate.3.slots_ref, bf16[5,384,128]{2,1,0:T(8,128)(2,1)S(1)} %copy-done.10, bf16[5,384,128]{2,1,0:T(8,128)(2,1)S(1)} %copy-done.12, bf16[5,384,128]{2,1,0:T(8,128)(2,1)S(1)} %get-tuple-element.57.refs_2_, ...), custom_call_target="tpu_custom_call" | custom-call | flops 1000000000 | bytes 1 | tf_op jit(solution)/shard_map/assemble/pallas_call | solution.py:241
  73.0 1.7 %collective-permute-done.7.first_ref = bf16[5,384,128]{2,1,0:T(8,128)(2,1)S(1)} collective-permute-done((bf16[5,384,128]{2,1,0:T(8,128)(2,1)S(1)}, bf16[5,384,128]{2,1,0:T(8,128)(2,1)S(1)}, u32[]{:S(2)}, u32[]{:S(2)}) %collective-permute-start.7) | collective-permute-done | bytes 491552 | tf_op jit(solution)/shard_map/ppermute | solution.py:300
  74.7 2.8 %complete.1 = bf16[384,40,128]{2,1,0:T(8,128)(2,1)} custom-call(s32[1]{0:T(128)} %bitcast.slot_ref, bf16[5,384,128]{2,1,0:T(8,128)(2,1)S(1)} %collective-permute-done.7.first_ref, bf16[5,384,128]{2,1,0:T(8,128)(2,1)} %collective-permute-done.12.second_ref, bf16[384,16,128]{2,1,0:T(8,128)(2,1)S(1)} %get-tuple-element.64.old_ref, ...), custom_call_target="tpu_custom_call", output_to_operand_aliasing={{}: (4, {})} | custom-call | tf_op jit(solution)/shard_map/complete/pallas_call | solution.py:278
  (45 shorter events, 6.1 us)
Async XLA Ops:
  4.9 29.2 %collective-permute-start = (bf16[21,384,128]{2,1,0:T(8,128)(2,1)}, bf16[21,384,128]{2,1,0:T(8,128)(2,1)S(1)}, u32[]{:S(2)}, u32[]{:S(2)}) collective-permute-start(bf16[21,384,128]{2,1,0:T(8,128)(2,1)} %get-tuple-element.35), channel_id=1, source_target_pairs={{0,1},{1,2},{2,3},{3,4},{4,5},{5,6},{6,7},{7,0},{8,9},{9,10},{10,1... | collective-permute-start | bytes 6193160 | tf_op jit(solution)/shard_map/ppermute | solution.py:25
  7.6 24.1 %collective-permute-start.2 = (bf16[2,5,384,128]{3,2,1,0:T(8,128)(2,1)}, bf16[2,5,384,128]{3,2,1,0:T(8,128)(2,1)}, u32[]{:S(2)}, u32[]{:S(2)}) collective-permute-start(bf16[2,5,384,128]{3,2,1,0:T(8,128)(2,1)} %get-tuple-element.39), channel_id=1, source_target_pairs={{0,8},{8,0},{16,24},{24,16},{1,9},{9,1},{17,25},{25,17},{2,10},{10... | collective-permute-start | bytes 2949128 | tf_op jit(solution)/shard_map/ppermute | solution.py:300
  8.9 24.1 %collective-permute-start.3 = (bf16[2,5,384,128]{3,2,1,0:T(8,128)(2,1)}, bf16[2,5,384,128]{3,2,1,0:T(8,128)(2,1)}, u32[]{:S(2)}, u32[]{:S(2)}) collective-permute-start(bf16[2,5,384,128]{3,2,1,0:T(8,128)(2,1)} %get-tuple-element.40), channel_id=1, source_target_pairs={{0,16},{16,0},{8,24},{24,8},{1,17},{17,1},{9,25},{25,9},{2,18},{18... | collective-permute-start | bytes 2949128 | tf_op jit(solution)/shard_map/ppermute | solution.py:300
  10.2 2.1 %copy-start.8 = (bf16[1,384,40,128]{3,2,1,0:T(8,128)(2,1)S(1)}, bf16[1,384,40,128]{3,2,1,0:T(8,128)(2,1)}, u32[]{:S(2)}) copy-start(bf16[1,384,40,128]{3,2,1,0:T(8,128)(2,1)} %param.5) | copy-start | bytes 11796484
  14.2 29.1 %copy-start.7 = (s32[384]{0:T(512)S(1)}, s32[384]{0:T(512)}, u32[]{:S(2)}) copy-start(s32[384]{0:T(512)} %param.8) | copy-start | bytes 4612
  20.3 22.0 %collective-permute-start.6 = (bf16[5,384,128]{2,1,0:T(8,128)(2,1)}, bf16[5,384,128]{2,1,0:T(8,128)(2,1)S(1)}, u32[]{:S(2)}, u32[]{:S(2)}) collective-permute-start(bf16[5,384,128]{2,1,0:T(8,128)(2,1)} %get-tuple-element.44), channel_id=1, source_target_pairs={{0,8},{8,0},{16,24},{24,16},{1,9},{9,1},{17,25},{25,17},{2,10},{10... | collective-permute-start | bytes 1474568 | tf_op jit(solution)/shard_map/ppermute | solution.py:300
  20.6 22.7 %collective-permute-start.5 = (bf16[5,384,128]{2,1,0:T(8,128)(2,1)}, bf16[5,384,128]{2,1,0:T(8,128)(2,1)}, u32[]{:S(2)}, u32[]{:S(2)}) collective-permute-start(bf16[5,384,128]{2,1,0:T(8,128)(2,1)} %get-tuple-element.41), channel_id=1, source_target_pairs={{0,16},{16,0},{8,24},{24,8},{1,17},{17,1},{9,25},{25,9},{2,18},{18... | collective-permute-start | bytes 1474568 | tf_op jit(solution)/shard_map/ppermute | solution.py:300
  31.8 22.8 %collective-permute-start.1 = (bf16[5,384,128]{2,1,0:T(8,128)(2,1)}, bf16[5,384,128]{2,1,0:T(8,128)(2,1)S(1)}, u32[]{:S(2)}, u32[]{:S(2)}) collective-permute-start(bf16[5,384,128]{2,1,0:T(8,128)(2,1)} %get-tuple-element.38), channel_id=1, source_target_pairs={{0,16},{16,0},{8,24},{24,8},{1,17},{17,1},{9,25},{25,9},{2,18},{18... | collective-permute-start | bytes 1474568 | tf_op jit(solution)/shard_map/ppermute | solution.py:300
  32.9 25.1 %collective-permute-start.8 = (bf16[5,384,128]{2,1,0:T(8,128)(2,1)}, bf16[5,384,128]{2,1,0:T(8,128)(2,1)S(1)}, u32[]{:S(2)}, u32[]{:S(2)}) collective-permute-start(bf16[5,384,128]{2,1,0:T(8,128)(2,1)} %get-tuple-element.52), channel_id=1, source_target_pairs={{0,8},{8,0},{16,24},{24,16},{1,9},{9,1},{17,25},{25,17},{2,10},{10... | collective-permute-start | bytes 1474568 | tf_op jit(solution)/shard_map/ppermute | solution.py:300
  34.1 16.5 %collective-permute-start.4 = (bf16[2,5,384,128]{3,2,1,0:T(8,128)(2,1)}, bf16[2,5,384,128]{3,2,1,0:T(8,128)(2,1)S(1)}, u32[]{:S(2)}, u32[]{:S(2)}) collective-permute-start(bf16[2,5,384,128]{3,2,1,0:T(8,128)(2,1)} %collective-permute-done.2), channel_id=1, source_target_pairs={{0,1},{1,2},{2,3},{3,4},{4,5},{5,6},{6,7},{7,0},{8,9},{9,10},{10,1... | collective-permute-start | bytes 2949128 | tf_op jit(solution)/shard_map/ppermute | solution.py:25
  42.3 15.7 %collective-permute-start.9 = (bf16[2,5,384,128]{3,2,1,0:T(8,128)(2,1)}, bf16[2,5,384,128]{3,2,1,0:T(8,128)(2,1)S(1)}, u32[]{:S(2)}, u32[]{:S(2)}) collective-permute-start(bf16[2,5,384,128]{3,2,1,0:T(8,128)(2,1)} %collective-permute-done.3), channel_id=1, source_target_pairs={{0,1},{1,2},{2,3},{3,4},{4,5},{5,6},{6,7},{7,0},{8,9},{9,10},{10,1... | collective-permute-start | bytes 2949128 | tf_op jit(solution)/shard_map/ppermute | solution.py:25
  43.3 1.6 %copy-start = (bf16[21,384,128]{2,1,0:T(8,128)(2,1)S(1)}, bf16[21,384,128]{2,1,0:T(8,128)(2,1)}, u32[]{:S(2)}) copy-start(bf16[21,384,128]{2,1,0:T(8,128)(2,1)} %get-tuple-element.35) | copy-start | bytes 6193156
  44.9 6.2 %copy-start.6 = (bf16[10,384,128]{2,1,0:T(8,128)(2,1)S(1)}, bf16[10,384,128]{2,1,0:T(8,128)(2,1)}, u32[]{:S(2)}) copy-start(bf16[10,384,128]{2,1,0:T(8,128)(2,1)} %copy-done.5) | copy-start | bytes 2949124
  49.4 18.6 %collective-permute-start.10 = (bf16[5,384,128]{2,1,0:T(8,128)(2,1)}, bf16[5,384,128]{2,1,0:T(8,128)(2,1)}, u32[]{:S(2)}, u32[]{:S(2)}) collective-permute-start(bf16[5,384,128]{2,1,0:T(8,128)(2,1)} %get-tuple-element.45), channel_id=1, source_target_pairs={{0,16},{16,0},{8,24},{24,8},{1,17},{17,1},{9,25},{25,9},{2,18},{18... | collective-permute-start | bytes 1474568 | tf_op jit(solution)/shard_map/ppermute | solution.py:300
  50.6 3.9 %copy-start.1 = (bf16[2,5,384,128]{3,2,1,0:T(8,128)(2,1)}, bf16[2,5,384,128]{3,2,1,0:T(8,128)(2,1)S(1)}, u32[]{:S(2)}) copy-start(bf16[2,5,384,128]{3,2,1,0:T(8,128)(2,1)S(1)} %collective-permute-done.4) | copy-start | bytes 2949124
  50.6 17.4 %collective-permute-start.11 = (bf16[5,384,128]{2,1,0:T(8,128)(2,1)}, bf16[5,384,128]{2,1,0:T(8,128)(2,1)}, u32[]{:S(2)}, u32[]{:S(2)}) collective-permute-start(bf16[5,384,128]{2,1,0:T(8,128)(2,1)} %get-tuple-element.60), channel_id=1, source_target_pairs={{0,8},{8,0},{16,24},{24,16},{1,9},{9,1},{17,25},{25,17},{2,10},{10... | collective-permute-start | bytes 1474568 | tf_op jit(solution)/shard_map/ppermute | solution.py:300
  54.5 6.2 %copy-start.11 = (bf16[5,384,128]{2,1,0:T(8,128)(2,1)}, bf16[5,384,128]{2,1,0:T(8,128)(2,1)S(1)}, u32[]{:S(2)}) copy-start(bf16[5,384,128]{2,1,0:T(8,128)(2,1)S(1)} %get-tuple-element.50.refs_1_) | copy-start | bytes 1474564
  57.5 5.2 %copy-start.2 = (bf16[2,5,384,128]{3,2,1,0:T(8,128)(2,1)S(1)}, bf16[2,5,384,128]{3,2,1,0:T(8,128)(2,1)}, u32[]{:S(2)}) copy-start(bf16[2,5,384,128]{3,2,1,0:T(8,128)(2,1)} %copy-done.1) | copy-start | bytes 2949124
  57.5 17.2 %collective-permute-start.7 = (bf16[5,384,128]{2,1,0:T(8,128)(2,1)S(1)}, bf16[5,384,128]{2,1,0:T(8,128)(2,1)S(1)}, u32[]{:S(2)}, u32[]{:S(2)}) collective-permute-start(bf16[5,384,128]{2,1,0:T(8,128)(2,1)S(1)} %attend.7), channel_id=1, source_target_pairs={{0,16},{16,0},{8,24},{24,8},{1,17},{17,1},{9,25},{25,9},{2,18},{18... | collective-permute-start | bytes 1474568 | tf_op jit(solution)/shard_map/ppermute | solution.py:300
  60.8 1.0 %copy-start.3 = (bf16[2,5,384,128]{3,2,1,0:T(8,128)(2,1)}, bf16[2,5,384,128]{3,2,1,0:T(8,128)(2,1)S(1)}, u32[]{:S(2)}) copy-start(bf16[2,5,384,128]{3,2,1,0:T(8,128)(2,1)S(1)} %collective-permute-done.9) | copy-start | bytes 2949124
  61.7 13.0 %collective-permute-start.12 = (bf16[5,384,128]{2,1,0:T(8,128)(2,1)S(1)}, bf16[5,384,128]{2,1,0:T(8,128)(2,1)}, u32[]{:S(2)}, u32[]{:S(2)}) collective-permute-start(bf16[5,384,128]{2,1,0:T(8,128)(2,1)S(1)} %attend.8), channel_id=1, source_target_pairs={{0,8},{8,0},{16,24},{24,16},{1,9},{9,1},{17,25},{25,17},{2,10},{10... | collective-permute-start | bytes 1474568 | tf_op jit(solution)/shard_map/ppermute | solution.py:300
  62.6 1.2 %copy-start.4 = (bf16[2,5,384,128]{3,2,1,0:T(8,128)(2,1)S(1)}, bf16[2,5,384,128]{3,2,1,0:T(8,128)(2,1)}, u32[]{:S(2)}) copy-start(bf16[2,5,384,128]{3,2,1,0:T(8,128)(2,1)} %copy-done.3) | copy-start | bytes 2949124
  63.8 4.2 %copy-start.10 = (bf16[5,384,128]{2,1,0:T(8,128)(2,1)S(1)}, bf16[5,384,128]{2,1,0:T(8,128)(2,1)}, u32[]{:S(2)}) copy-start(bf16[5,384,128]{2,1,0:T(8,128)(2,1)} %copy-done.9) | copy-start | bytes 1474564
  63.8 4.2 %copy-start.12 = (bf16[5,384,128]{2,1,0:T(8,128)(2,1)S(1)}, bf16[5,384,128]{2,1,0:T(8,128)(2,1)}, u32[]{:S(2)}) copy-start(bf16[5,384,128]{2,1,0:T(8,128)(2,1)} %copy-done.11) | copy-start | bytes 1474564
  (4 other events, 3.6 us)

commit v3 on v2

--- a/solution.py
+++ b/solution.py
@@ -12,8 +12,6 @@
 ACROSS_Y = ((0, 2), (2, 0), (1, 3), (3, 1))
 BLOCK = 128
 ROWS = 8
-ID_BASE = 256
-ID_ROWS = 16
 PARAMS = pltpu.CompilerParams(vmem_limit_bytes=12 * 2**20)
 IN_VMEM = pl.BlockSpec(memory_space=pltpu.VMEM)
 IN_SMEM = pl.BlockSpec(memory_space=pltpu.SMEM)
@@ -29,32 +27,17 @@
     return (values * cosine + pltpu.roll(values, values.shape[-1] // 2, 1) * sine).astype(jnp.bfloat16)
 
 
-def prepare_cache(keys_values, positions, documents):
-    tokens, _, heads, head_dim = keys_values.shape
-    half = heads // 2
+def prepare_cache(raws, positions=None, tables=None):
+    tokens, head_dim = raws[0].shape[0], raws[0].shape[-1]
     half_dim = head_dim // 2
     steps = tokens // BLOCK
-    chunk = BLOCK * heads * 2
-    rows = jnp.transpose(keys_values, (0, 2, 1, 3)).reshape(tokens * heads * 2, head_dim)
+    counts = [raw.shape[2] for raw in raws]
+    rows = [jnp.transpose(raw, (0, 2, 1, 3)).reshape(-1, head_dim) for raw in raws]
     exponent = np.arange(half_dim, dtype=np.float32) * np.float32(2.0 / head_dim)
     inverse = np.power(np.float32(10000.0), -exponent).astype(np.float32)
     inverse = jnp.asarray(np.concatenate([inverse, inverse])[None])
 
-    def kernel(positions_hbm, documents_hbm, inverse_hbm, rows_ref, all_ref, a_ref, b_ref, cosine_ref, sine_ref, *scratch):
-        positions_ref, documents_ref, inverse_ref, ids, landed, wide, done, small_sems, row_sems, store_sems = scratch
-        small = [
-            pltpu.make_async_copy(positions_hbm, positions_ref, small_sems.at[0]),
-            pltpu.make_async_copy(documents_hbm, documents_ref, small_sems.at[1]),
-            pltpu.make_async_copy(inverse_hbm, inverse_ref, small_sems.at[2]),
-        ]
-        copies = [
-            pltpu.make_async_copy(rows_ref.at[pl.ds(i * chunk, chunk)], landed.at[i], row_sems.at[i])
-            for i in range(steps)
-        ]
-        for copy in (*small, *copies):
-            copy.start()
-        for copy in small:
-            copy.wait()
+    def fill_tables(positions_ref, inverse_ref, cosine_ref, sine_ref):
         left = lax.broadcasted_iota(jnp.int32, (BLOCK, head_dim), 1) < half_dim
         columns = [
             jnp.transpose(jnp.broadcast_to(positions_ref[i : i + 1], (BLOCK, BLOCK))).astype(jnp.float32)
@@ -75,65 +58,37 @@
                     at = slice((i + k) * BLOCK, (i + k + 1) * BLOCK)
                     cosine_ref[at] = c
                     sine_ref[at] = s
-        ids[...] = jnp.concatenate(
-            [
-                documents_ref[...] // ID_BASE,
-                documents_ref[...] % ID_BASE,
-                jnp.zeros((ID_ROWS - 2 * steps, BLOCK), jnp.int32),
-            ],
-            axis=0,
-        ).astype(jnp.float32).astype(jnp.bfloat16)
-        stores = [
-            pltpu.make_async_copy(ids, all_ref.at[2 * heads, pl.ds(0, ID_ROWS)], store_sems.at[0])
-        ]
-        stores[0].start()
-        for i in range(steps):
-            at = slice(i * BLOCK, (i + 1) * BLOCK)
-            copies[i].wait()
-            wide[...] = landed[i].astype(jnp.float32)
+
+    def kernel(*refs):
+        *refs, wide = refs
+        row_refs, refs = refs[: len(rows)], refs[len(rows) :]
+        (first, second), out_refs = refs[:2], refs[2 : 2 + len(rows)]
+        if tables is None:
+            cosine_ref, sine_ref = refs[-2:]
+            fill_tables(first, second, cosine_ref, sine_ref)
+        else:
+            cosine_ref, sine_ref = first, second
+        for heads, row_ref, out_ref in zip(counts, row_refs, out_refs):
+            wide[: 2 * heads * tokens] = row_ref[...].astype(jnp.float32)
             for head in range(heads):
-                key = wide[pl.ds(2 * head, BLOCK, stride=2 * heads), :]
-                done[i, head] = turn(key, cosine_ref[at], sine_ref[at])
-                done[i, heads + head] = wide[pl.ds(2 * head + 1, BLOCK, stride=2 * heads), :].astype(jnp.bfloat16)
-            rows_at = pl.ds(i * BLOCK, BLOCK)
-            moves = [(done.at[i], all_ref.at[pl.ds(0, 2 * heads), rows_at])]
-            for k in range(2):
-                moves.append((done.at[i, pl.ds(k * heads, half)], a_ref.at[k, :, rows_at]))
-                moves.append((done.at[i, pl.ds(k * heads + half, heads - half)], b_ref.at[k, :, rows_at]))
-            for source, target in moves:
-                store = pltpu.make_async_copy(source, target, store_sems.at[len(stores)])
-                store.start()
-                stores.append(store)
-        for store in stores:
-            store.wait()
-
-    table = jax.ShapeDtypeStruct((tokens, head_dim), jnp.float32)
-    anywhere = pl.BlockSpec(memory_space=pl.ANY)
-    return pl.pallas_call(
-        kernel,
-        in_specs=[anywhere] * 4,
-        out_specs=[anywhere] * 3 + [IN_VMEM] * 2,
-        out_shape=[
-            jax.ShapeDtypeStruct((2 * heads + 1, tokens, head_dim), jnp.bfloat16),
-            *(jax.ShapeDtypeStruct((2, n, tokens, head_dim), jnp.bfloat16) for n in (half, heads - half)),
-            table,
-            table,
-        ],
-        scratch_shapes=[
-            pltpu.VMEM((steps, BLOCK), jnp.int32),
-            pltpu.VMEM((steps, BLOCK), jnp.int32),
-            pltpu.VMEM((1, head_dim), jnp.float32),
-            pltpu.VMEM((ID_ROWS, BLOCK), jnp.bfloat16),
-            pltpu.VMEM((steps, chunk, head_dim), jnp.bfloat16),
-            pltpu.VMEM((chunk, head_dim), jnp.float32),
-            pltpu.VMEM((steps, 2 * heads, BLOCK, head_dim), jnp.bfloat16),
-            pltpu.SemaphoreType.DMA((3,)),
-            pltpu.SemaphoreType.DMA((steps,)),
-            pltpu.SemaphoreType.DMA((1 + 5 * steps,)),
-        ],
-        compiler_params=pltpu.CompilerParams(vmem_limit_bytes=60 * 2**20),
+                key = wide[pl.ds(2 * head, tokens, stride=2 * heads), :]
+                out_ref[0, head] = turn(key, cosine_ref[...], sine_ref[...])
+                value = wide[pl.ds(2 * head + 1, tokens, stride=2 * heads), :]
+                out_ref[1, head] = value.astype(jnp.bfloat16)
+
+    out_shape = [jax.ShapeDtypeStruct((2, n, tokens, head_dim), jnp.bfloat16) for n in counts]
+    if tables is None:
+        out_shape += [jax.ShapeDtypeStruct((tokens, head_dim), jnp.float32)] * 2
+    return pl.pallas_call(
+        kernel,
+        in_specs=[IN_VMEM] * (len(rows) + 2),
+        out_specs=[IN_VMEM] * len(out_shape),
+        out_shape=out_shape,
+        scratch_shapes=[pltpu.VMEM((2 * max(counts) * tokens, head_dim), jnp.float32)],
+        compiler_params=PARAMS,
+        cost_estimate=pl.CostEstimate(flops=1, bytes_accessed=1, transcendentals=0),
         name="prepare_cache",
-    )(positions.reshape(steps, BLOCK), documents.reshape(steps, BLOCK), inverse, rows)
+    )(*rows, *((positions.reshape(steps, BLOCK), inverse) if tables is None else tables))
 
 
 def prepare_queries(queries, cosine, sine, starts, counts):
@@ -233,21 +188,25 @@
         outs[0][...] = jnp.swapaxes(gathered[...], 0, 1)
         if window:
             first = pl.multiple_of(slots_ref[len(pieces)] * ROWS, ROWS)
-            outs[1][...] = jnp.swapaxes(gathered[pl.ds(first, window)], 0, 1)
+            outs[1][...] = gathered[pl.ds(first, window)]
 
     if window:
         slots = jnp.concatenate([slots, window_start[None]])
-    counts = (heads, window) if window else (heads,)
+    out_specs = [pl.BlockSpec((step, heads, head_dim), lambda i, s: (i, 0, 0))]
+    out_shape = [jax.ShapeDtypeStruct((tokens, heads, head_dim), jnp.bfloat16)]
+    if window:
+        out_specs.append(pl.BlockSpec((window, step, head_dim), lambda i, s: (0, i, 0)))
+        out_shape.append(jax.ShapeDtypeStruct((window, tokens, head_dim), jnp.bfloat16))
     return pl.pallas_call(
         kernel,
         grid_spec=pltpu.PrefetchScalarGridSpec(
             num_scalar_prefetch=1,
             grid=(tokens // step,),
             in_specs=[pl.BlockSpec((count, step, head_dim), lambda i, s: (0, i, 0))] * len(pieces),
-            out_specs=[pl.BlockSpec((step, n, head_dim), lambda i, s: (i, 0, 0)) for n in counts],
+            out_specs=out_specs,
             scratch_shapes=[pltpu.VMEM((heads, step, head_dim), jnp.bfloat16)],
         ),
-        out_shape=[jax.ShapeDtypeStruct((tokens, n, head_dim), jnp.bfloat16) for n in counts],
+        out_shape=out_shape,
         compiler_params=PARAMS,
         cost_estimate=pl.CostEstimate(flops=10**9, bytes_accessed=1, transcendentals=0),
         name="assemble",
@@ -257,39 +216,38 @@
 def complete(gathered, old, pieces, slot):
     count, tokens, head_dim = pieces[0].shape
     mine = 2 * count
-    window = old.shape[1]
-
-    def kernel(slot_ref, first_ref, second_ref, old_ref, _, out_ref, placed):
-        j = pl.program_id(0)
+    window = old.shape[0]
+
+    steps = tokens // BLOCK
+
+    def kernel(slot_ref, first_ref, second_ref, old_ref, _, out_ref, placed, ready, sems):
         block = (slot_ref[0] * mine) // ROWS
         low = slot_ref[0] * mine - block * ROWS
-
-        @pl.when(j == 0)
-        def _():
-            placed[pl.ds(low, count)] = first_ref[...]
-            placed[pl.ds(low + count, count)] = second_ref[...]
-
-        row = lax.broadcasted_iota(jnp.int32, (tokens, ROWS, head_dim), 1) + j * ROWS
-        new = jnp.swapaxes(placed[pl.ds(pl.multiple_of(j * ROWS, ROWS), ROWS)], 0, 1)
-        keep = jnp.logical_or(row < low, row >= low + mine)
-        out_ref[...] = jnp.where(keep, old_ref[...], new)
-
-    piece = pl.BlockSpec((count, tokens, head_dim), lambda j, s: (0, 0, 0))
-    return pl.pallas_call(
-        kernel,
-        grid_spec=pltpu.PrefetchScalarGridSpec(
-            num_scalar_prefetch=1,
-            grid=(window // ROWS,),
-            in_specs=[
-                piece,
-                piece,
-                pl.BlockSpec((tokens, ROWS, head_dim), lambda j, s: (0, j, 0)),
-                pl.BlockSpec(memory_space=pl.ANY),
-            ],
-            out_specs=pl.BlockSpec((tokens, ROWS, head_dim), lambda j, s: (0, (s[0] * mine) // ROWS + j, 0)),
-            scratch_shapes=[pltpu.VMEM((window, tokens, head_dim), jnp.bfloat16)],
-        ),
+        placed[...] = old_ref[...]
+        placed[pl.ds(low, count)] = first_ref[...]
+        placed[pl.ds(low + count, count)] = second_ref[...]
+        heads_at = pl.ds(pl.multiple_of(block * ROWS, ROWS), window)
+        copies = []
+        for i in range(steps):
+            at = slice(i * BLOCK, (i + 1) * BLOCK)
+            ready[at] = jnp.swapaxes(placed[:, at], 0, 1)
+            at = pl.ds(i * BLOCK, BLOCK)
+            copies.append(pltpu.make_async_copy(ready.at[at], out_ref.at[at, heads_at], sems.at[i]))
+            copies[i].start()
+        for copy in copies:
+            copy.wait()
+
+    anywhere = pl.BlockSpec(memory_space=pl.ANY)
+    return pl.pallas_call(
+        kernel,
+        in_specs=[IN_SMEM, IN_VMEM, IN_VMEM, IN_VMEM, anywhere],
+        out_specs=anywhere,
         out_shape=jax.ShapeDtypeStruct(gathered.shape, gathered.dtype),
+        scratch_shapes=[
+            pltpu.VMEM((window, tokens, head_dim), jnp.bfloat16),
+            pltpu.VMEM((tokens, window, head_dim), jnp.bfloat16),
+            pltpu.SemaphoreType.DMA((steps,)),
+        ],
         input_output_aliases={4: 0},
         compiler_params=PARAMS,
         name="complete",
@@ -313,11 +271,12 @@
     half = mine // 2
     section = lax.axis_index("section")
     beside_x, beside_y, opposite = section ^ 1, section ^ 2, section ^ 3
-    tokens = documents.shape[0]
-    share, share_a, share_b, cosine, sine = prepare_cache(keys_values, positions, documents)
-    cache_a = across(share_a, ACROSS_X)
-    cache_b = across(share_b, ACROSS_Y)
-    before = shifted(share, "ctx")
+    part_a, part_b = keys_values[:, :, :half], keys_values[:, :, half:]
+    raw_a = across(part_a, ACROSS_X)
+    raw_b = across(part_b, ACROSS_Y)
+    raw_before = shifted(keys_values, "ctx")
+    labels = shifted(jnp.stack([positions, documents]), "ctx")
+    share, cosine, sine = prepare_cache((keys_values,), positions)
 
     starts = jnp.stack(
         [
@@ -335,32 +294,34 @@
     )
     near_a = across(near_y, ACROSS_Y)
     near_b = across(near_x, ACROSS_X)
-    cache_a, cache_b = after((cache_a, cache_b), (near_y, before))
-    earlier_a = shifted(cache_a, "ctx")
-    earlier_b = shifted(cache_b, "ctx")
+    raw_a, raw_b = after((raw_a, raw_b), (near_y, raw_before))
+    raw_earlier_a = shifted(raw_a, "ctx")
+    raw_earlier_b = shifted(after(raw_b, near_a), "ctx")
     far_a = across(far_y, ACROSS_Y)
     far_b = across(far_x, ACROSS_X)
 
-    blocks = tokens // BLOCK
-    ids = before[2 * mine].astype(jnp.int32)
+    before, *earlier_tables = prepare_cache((raw_before,), labels[0])
+    earlier_docs = jnp.where(lax.axis_index("ctx") == 0, -1, labels[1])
+    cache_a, cache_b = prepare_cache((raw_a, raw_b), tables=(cosine, sine))
+    near_a, near_b = after((near_a, near_b), (before, cache_a))
     share, before = rows_of(share), rows_of(before)
-    earlier_docs = ids[:blocks] * ID_BASE + ids[blocks : 2 * blocks]
-    earlier_docs = jnp.where(lax.axis_index("ctx") == 0, -1, earlier_docs)
     near = (((share, 0, mine), (before, 0, mine)), ((share, half, mine), (before, half, mine)))
     out_near_a, out_near_b = attend(
         (((near_a, 0, half), *near[0]), ((near_b, 0, half), *near[1])), documents, earlier_docs, 5 * 10**10
     )
     back_near_a = across(out_near_a, ACROSS_Y)
-    back_near_b = across(after(out_near_b, earlier_a), ACROSS_X)
+    back_near_b = across(after(out_near_b, raw_earlier_a), ACROSS_X)
     own_near = after(own_near, out_near_a)
     own_near_a, own_near_b = attend(
         (((own_near, 0, half), *near[0]), ((own_near, half, half), *near[1])), documents, earlier_docs
     )
-    far_a, earlier_a = after((far_a, earlier_a), own_near_a)
+    far_a, raw_earlier_a = after((far_a, raw_earlier_a), own_near_a)
+    (earlier_a,) = prepare_cache((raw_earlier_a,), tables=earlier_tables)
     far_of_a = tuple((rows_of(c), 0, half) for c in (cache_a, earlier_a))
     (out_far_a,) = attend((((far_a, 0, half), *far_of_a),), documents, earlier_docs)
     back_far_a = across(out_far_a, ACROSS_Y)
-    far_b, earlier_b = after((far_b, earlier_b), out_far_a)
+    far_b, raw_earlier_b = after((far_b, raw_earlier_b), out_far_a)
+    (earlier_b,) = prepare_cache((raw_earlier_b,), tables=earlier_tables)
     far_of_b = tuple((rows_of(c), 0, half) for c in (cache_b, earlier_b))
     (out_far_b,) = attend((((far_b, 0, half), *far_of_b),), documents, earlier_docs)
     back_far_b = across(out_far_b, ACROSS_X)
@@ -386,8 +347,7 @@
     mine = keys_values.shape[2]
     earlier_docs = shifted(documents, "ctx")
     earlier_docs = jnp.where(lax.axis_index("ctx") == 0, -1, earlier_docs)
-    share, _, _, cosine, sine = prepare_cache(keys_values, positions, documents)
-    share = share[:-1].reshape(2, mine, *share.shape[1:])
+    share, cosine, sine = prepare_cache((keys_values,), positions)
     whole = lax.all_gather(share, "section", axis=1, tiled=True)
     earlier = shifted(whole, "ctx")
     starts = jnp.zeros((1,), jnp.int32)

time: 78.7 us -> 76.8 us (0.976)
  waiting for transfers between devices: 20.6 us -> 16 us
  starting transfers between devices: 12.2 us -> 15.6 us
    ppermute x10, waiting for transfers between devices: 20.6 us -> 10.9 us  [across(): return lax.ppermute(value, 'section', route)]
    ppermute x3 -> x4, waiting for transfers between devices: 0.01 us -> 5.05 us  [shifted(): return lax.ppermute(block, axis, [(i, (i + 1) % size) for i in range(size)])]
    unnamed x30, local copies, waits for them, and re-layouts: 9.45 us -> 5.83 us
    slice x0 -> x1, local copies, waits for them, and re-layouts: none -> 3.49 us  [square_body(): part_a, part_b = (keys_values[:, :, :half], keys_values[:, :, half:])]
    pallas_call x5, Pallas kernels: 17 us -> 14.1 us  [attend(): pl.pallas_call(kernel, in_specs=[IN_VMEM] * (2 + 3 * n), out_specs=[IN_VM...]
    pallas_call x2 -> x6, Pallas kernels: 7.67 us -> 10.4 us  [the longest x5 7.64 us: prepare_cache(): pl.pallas_call(kernel, in_specs=[IN_VMEM] * (len(rows) + 2), out_specs=[I...]
    ppermute x3 -> x4, starting transfers between devices: 3.9 us -> 6.24 us  [shifted(): return lax.ppermute(block, axis, [(i, (i + 1) % size) for i in range(size)])]
    ppermute x10, starting transfers between devices: 8.3 us -> 9.41 us  [across(): return lax.ppermute(value, 'section', route)]
  transfers between devices with their start and end apart: 13 -> 14, of which waited for: 4 -> 6; matrix products, arithmetic and copies ran while one was open for 0% -> 5% of each run, Pallas kernels for 35% -> 42%
where the time goes in v3:
time: 76.8 us; the launch traced here: 76.1 us
  Pallas kernels  34.6 us (45%)
  waiting for transfers between devices  16 us (21%)
  starting transfers between devices  15.6 us (20%)
  local copies, waits for them, and re-layouts  9.49 us (12%)
    pallas_call x5, Pallas kernels, attend(): pl.pallas_call(kernel, in_specs=[IN_VMEM] * (2 + 3 * n), out_specs=[IN_VM...  14.1 us
    ppermute x10, waiting for transfers between devices, across(): return lax.ppermute(value, 'section', route)  10.9 us
    ppermute x10, starting transfers between devices, across(): return lax.ppermute(value, 'section', route)  9.41 us
    pallas_call x5, Pallas kernels, prepare_cache(): pl.pallas_call(kernel, in_specs=[IN_VMEM] * (len(rows) + 2), out_specs=[I...  7.64 us
    ppermute x4, starting transfers between devices, shifted(): return lax.ppermute(block, axis, [(i, (i + 1) % size) for i in range(size)])  6.24 us
    unnamed x30, local copies, waits for them, and re-layouts  5.83 us
    pallas_call x1, Pallas kernels, prepare_queries(): pl.pallas_call(kernel, in_specs=[IN_SMEM] + [IN_VMEM] * 3, out_specs=[IN_...  5.06 us
    pallas_call x1, Pallas kernels, assemble(): pl.pallas_call(kernel, grid_spec=pltpu.PrefetchScalarGridSpec(num_scalar_...  5.05 us
  transfers between devices with their start and end apart: 14, of which 6 were waited for; matrix products, arithmetic and copies ran while one was open for 5% of the time, Pallas kernels for 42%

profile of v3, /device:TPU:1, one launch (start us, length us, event | category | flops | bytes accessed | tf_op | source)
XLA Modules:
  0.0 76.1 jit_solution(4784574821450139864)
XLA Ops:
  0.0 2.7 %collective-permute-start.4 = (bf16[384,2,10,128]{3,1,2,0:T(2,128)(2,1)}, bf16[384,2,10,128]{3,1,2,0:T(2,128)(2,1)}, u32[]{:S(2)}, u32[]{:S(2)}) collective-permute-start(bf16[384,2,10,128]{3,1,2,0:T(2,128)(2,1)} %param.7), channel_id=1, source_target_pairs={{0,1},{1,2},{2,3},{3,4},{4,5},{5,6},{6,7},{7,0},{8,9},{9,10},{10,1... | collective-permute-start | bytes 5898248 | tf_op jit(solution)/shard_map/ppermute | solution.py:23
  2.8 3.5 %fusion.1 = (bf16[384,2,5,128]{3,1,2,0:T(2,128)(2,1)}, bf16[384,2,5,128]{3,1,2,0:T(2,128)(2,1)}) fusion(bf16[384,2,10,128]{3,1,2,0:T(2,128)(2,1)} %param.7), kind=kLoop, calls=%fused_computation.4 | loop fusion | bytes 3932160 | tf_op jit(solution)/shard_map/slice | solution.py:274
  7.5 1.2 %collective-permute-start.3 = (bf16[384,2,5,128]{3,1,2,0:T(2,128)(2,1)}, bf16[384,2,5,128]{3,1,2,0:T(2,128)(2,1)}, u32[]{:S(2)}, u32[]{:S(2)}) collective-permute-start(bf16[384,2,5,128]{3,1,2,0:T(2,128)(2,1)} %get-tuple-element.79), channel_id=1, source_target_pairs={{0,16},{16,0},{8,24},{24,8},{1,17},{17,1},{9,25},{25,9},{2,18},{18... | collective-permute-start | bytes 2949128 | tf_op jit(solution)/shard_map/ppermute | solution.py:258
  9.5 1.3 %prepare_cache.5 = (bf16[2,10,384,128]{3,2,1,0:T(8,128)(2,1)S(1)}, f32[384,128]{1,0:T(8,128)S(1)}, f32[384,128]{1,0:T(8,128)S(1)}) custom-call(bf16[7680,128]{1,0:T(8,128)(2,1)S(1)} %bitcast.49, s32[3,128]{1,0:T(4,128)S(1)} %bitcast.74, f32[1,128]{1,0:T(1,128)S(1)} %copy-done.9), custom_call_target="tpu_custom_call" | custom-call | flops 1 | bytes 1 | tf_op jit(solution)/shard_map/prepare_cache/pallas_call | solution.py:82
  10.9 1.3 %copy-done.1 = bf16[2,10,384,128]{3,2,1,0:T(8,128)(2,1)} copy-done((bf16[2,10,384,128]{3,2,1,0:T(8,128)(2,1)}, bf16[2,10,384,128]{3,2,1,0:T(8,128)(2,1)S(1)}, u32[]{:S(2)}) %copy-start.1) | copy-done | bytes 1966104
  12.2 2.1 %copy-done.10 = bf16[1,384,40,128]{3,2,1,0:T(8,128)(2,1)S(1)} copy-done((bf16[1,384,40,128]{3,2,1,0:T(8,128)(2,1)S(1)}, bf16[1,384,40,128]{3,2,1,0:T(8,128)(2,1)}, u32[]{:S(2)}) %copy-start.10) | copy-done | bytes 3932184
  14.3 5.1 %prepare_queries.1 = (bf16[5,384,128]{2,1,0:T(8,128)(2,1)}, bf16[5,384,128]{2,1,0:T(8,128)(2,1)}, bf16[5,384,128]{2,1,0:T(8,128)(2,1)}, bf16[5,384,128]{2,1,0:T(...) custom-call(s32[7]{0:T(128)S(1)} %stack.61.starts_ref, ...), custom_call_target="tpu_custom_call" | custom-call | flops 2000000000 | bytes 7864320 | tf_op jit(solution)/shard_map/prepare_queries/pallas_call | solution.py:111
  19.6 5.0 %collective-permute-done = s32[2,384]{1,0:T(2,128)S(1)} collective-permute-done((s32[2,384]{1,0:T(2,128)S(1)}, s32[2,384]{1,0:T(2,128)S(1)}, u32[]{:S(2)}, u32[]{:S(2)}) %collective-permute-start) | collective-permute-done | bytes 3104 | tf_op jit(solution)/shard_map/ppermute | solution.py:23
  25.9 3.4 %collective-permute-done.2 = bf16[384,2,5,128]{3,1,2,0:T(2,128)(2,1)} collective-permute-done((bf16[384,2,5,128]{3,1,2,0:T(2,128)(2,1)}, bf16[384,2,5,128]{3,1,2,0:T(2,128)(2,1)}, u32[]{:S(2)}, u32[]{:S(2)}) %collective-permute-start.2) | collective-permute-done | bytes 983072 | tf_op jit(solution)/shard_map/ppermute | solution.py:258
  29.2 1.8 %collective-permute-start.1 = (bf16[5,384,128]{2,1,0:T(8,128)(2,1)}, bf16[5,384,128]{2,1,0:T(8,128)(2,1)S(1)}, u32[]{:S(2)}, u32[]{:S(2)}) collective-permute-start(bf16[5,384,128]{2,1,0:T(8,128)(2,1)} %get-tuple-element.43), channel_id=1, source_target_pairs={{0,16},{16,0},{8,24},{24,8},{1,17},{17,1},{9,25},{25,9},{2,18},{18... | collective-permute-start | bytes 1474568 | tf_op jit(solution)/shard_map/ppermute | solution.py:258
  32.2 1.6 %collective-permute-start.5 = (bf16[384,2,5,128]{3,1,2,0:T(2,128)(2,1)}, bf16[384,2,5,128]{3,1,2,0:T(2,128)(2,1)S(1)}, u32[]{:S(2)}, u32[]{:S(2)}) collective-permute-start(bf16[384,2,5,128]{3,1,2,0:T(2,128)(2,1)} %collective-permute-done.2), channel_id=1, source_target_pairs={{0,1},{1,2},{2,3},{3,4},{4,5},{5,6},{6,7},{7,0},{8,9},{9,10},{10,1... | collective-permute-start | bytes 2949128 | tf_op jit(solution)/shard_map/ppermute | solution.py:23
  33.9 3.1 %prepare_cache.6 = (bf16[2,10,384,128]{3,2,1,0:T(8,128)(2,1)S(1)}, f32[384,128]{1,0:T(8,128)S(1)}, f32[384,128]{1,0:T(8,128)S(1)}) custom-call(bf16[7680,128]{1,0:T(8,128)(2,1)} %bitcast.14.refs_0_, s32[3,128]{1,0:T(4,128)S(1)} %bitcast.75, f32[1,128]{1,0:T(1,128)S(1)} %copy-done.9), custom_call_target="tpu_custom_call" | custom-call | flops 1 | bytes 1 | tf_op jit(solution)/shard_map/prepare_cache/pallas_call | solution.py:82
  36.9 2.3 %prepare_cache.7 = (bf16[2,5,384,128]{3,2,1,0:T(8,128)(2,1)S(1)}, bf16[2,5,384,128]{3,2,1,0:T(8,128)(2,1)S(1)}) custom-call(bf16[3840,128]{1,0:T(8,128)(2,1)} %bitcast.16.refs_0_, bf16[3840,128]{1,0:T(8,128)(2,1)} %bitcast.18.refs_1_, f32[384,128]{1,0:T(8,128)S(1)} %get-tuple-element.41.cosine_ref.refs_2_, f32[384,128]{1,0:T(8,128)S(1)} %get-tuple-element.42.sine_ref.refs_3_), custom_call_target="tpu_custom_call" | custom-call | flops 1 | bytes 1 | tf_op jit(solution)/shard_map/prepare_cache/pallas_call | solution.py:82
  39.3 2.7 %collective-permute-done.6.refs_0_ = bf16[5,384,128]{2,1,0:T(8,128)(2,1)} collective-permute-done((bf16[5,384,128]{2,1,0:T(8,128)(2,1)}, bf16[5,384,128]{2,1,0:T(8,128)(2,1)}, u32[]{:S(2)}, u32[]{:S(2)}) %collective-permute-start.6) | collective-permute-done | bytes 491552 | tf_op jit(solution)/shard_map/ppermute | solution.py:258
  43.1 4.8 %attend.5 = (bf16[5,384,128]{2,1,0:T(8,128)(2,1)}, bf16[5,384,128]{2,1,0:T(8,128)(2,1)}) custom-call(s32[3,128]{1,0:T(4,128)S(1)} %bitcast.64, s32[3,128]{1,0:T(4,128)S(1)} %bitcast.69, bf16[5,384,128]{2,1,0:T(8,128)(2,1)} %collective-permute-done.6.refs_0_, bf16[7680,128]{1,0:T(8,128)(2,1)S(1)} %bitcast.50, bf16[7680,128]{1,0:T(8,128)(2,1)S(1)} %bitcast.54, ...), custom_call_target="tpu_custom_call" | custom-call | flops 49999998976 | bytes 1 | tf_op jit(solution)/shard_map/attend/pallas_call | solution.py:168
  47.9 1.2 %collective-permute-start.11 = (bf16[5,384,128]{2,1,0:T(8,128)(2,1)}, bf16[5,384,128]{2,1,0:T(8,128)(2,1)}, u32[]{:S(2)}, u32[]{:S(2)}) collective-permute-start(bf16[5,384,128]{2,1,0:T(8,128)(2,1)} %get-tuple-element.54), channel_id=1, source_target_pairs={{0,16},{16,0},{8,24},{24,8},{1,17},{17,1},{9,25},{25,9},{2,18},{18... | collective-permute-start | bytes 1474568 | tf_op jit(solution)/shard_map/ppermute | solution.py:258
  49.4 2.8 %attend.6 = (bf16[5,384,128]{2,1,0:T(8,128)(2,1)S(1)}, bf16[5,384,128]{2,1,0:T(8,128)(2,1)S(1)}) custom-call(s32[3,128]{1,0:T(4,128)S(1)} %bitcast.65, s32[3,128]{1,0:T(4,128)S(1)} %bitcast.70, bf16[10,384,128]{2,1,0:T(8,128)(2,1)S(1)} %get-tuple-element.55.refs_0_.refs_3_, bf16[7680,128]{1,0:T(8,128)(2,1)S(1)} %bitcast.52, bf16[7680,128]{1,0:T(8,128)(2,1)S(1)} %bitcast.56, ...), custom_call_target="tpu_custom_call" | custom-call | flops 1 | bytes 1 | tf_op jit(solution)/shard_map/attend/pallas_call | solution.py:168
  53.1 1.5 %attend.7 = bf16[5,384,128]{2,1,0:T(8,128)(2,1)S(1)} custom-call(s32[3,128]{1,0:T(4,128)S(1)} %bitcast.66, s32[3,128]{1,0:T(4,128)S(1)} %bitcast.71, bf16[5,384,128]{2,1,0:T(8,128)(2,1)S(1)} %collective-permute-done.1.refs_0_, bf16[3840,128]{1,0:T(8,128)(2,1)S(1)} %bitcast.58, bf16[3840,128]{1,0:T(8,128)(2,1)S(1)} %bitcast.45), custom_call_target="tpu_custom_call" | custom-call | flops 1 | bytes 1 | tf_op jit(solution)/shard_map/attend/pallas_call | solution.py:168
  54.6 1.3 %collective-permute-start.8 = (bf16[5,384,128]{2,1,0:T(8,128)(2,1)S(1)}, bf16[5,384,128]{2,1,0:T(8,128)(2,1)}, u32[]{:S(2)}, u32[]{:S(2)}) collective-permute-start(bf16[5,384,128]{2,1,0:T(8,128)(2,1)S(1)} %attend.7), channel_id=1, source_target_pairs={{0,16},{16,0},{8,24},{24,8},{1,17},{17,1},{9,25},{25,9},{2,18},{18... | collective-permute-start | bytes 1474568 | tf_op jit(solution)/shard_map/ppermute | solution.py:258
  56.4 2.4 %attend.8 = bf16[5,384,128]{2,1,0:T(8,128)(2,1)} custom-call(s32[3,128]{1,0:T(4,128)S(1)} %bitcast.67, s32[3,128]{1,0:T(4,128)S(1)} %bitcast.72, bf16[5,384,128]{2,1,0:T(8,128)(2,1)S(1)} %collective-permute-done.9.refs_0_, bf16[3840,128]{1,0:T(8,128)(2,1)S(1)} %bitcast.60, bf16[3840,128]{1,0:T(8,128)(2,1)S(1)} %bitcast.47), custom_call_target="tpu_custom_call" | custom-call | flops 1 | bytes 1 | tf_op jit(solution)/shard_map/attend/pallas_call | solution.py:168
  61.5 2.7 %attend.9 = (bf16[5,384,128]{2,1,0:T(8,128)(2,1)S(1)}, bf16[5,384,128]{2,1,0:T(8,128)(2,1)S(1)}) custom-call(s32[3,128]{1,0:T(4,128)S(1)} %bitcast.68, s32[3,128]{1,0:T(4,128)S(1)} %bitcast.73, bf16[10,384,128]{2,1,0:T(8,128)(2,1)S(1)} %get-tuple-element.68.refs_0_.refs_3_, bf16[3840,128]{1,0:T(8,128)(2,1)S(1)} %bitcast.59, bf16[3840,128]{1,0:T(8,128)(2,1)S(1)} %bitcast.46, ...), custom_call_target="tpu_custom_call" | custom-call | flops 1 | bytes 1 | tf_op jit(solution)/shard_map/attend/pallas_call | solution.py:168
  64.2 5.0 %assemble.1 = (bf16[384,40,128]{2,1,0:T(8,128)(2,1)}, bf16[16,384,128]{2,1,0:T(8,128)(2,1)S(1)}) custom-call(s32[7]{0:T(128)S(1)} %concatenate.3.slots_ref, bf16[5,384,128]{2,1,0:T(8,128)(2,1)S(1)} %copy-done.12, bf16[5,384,128]{2,1,0:T(8,128)(2,1)S(1)} %copy-done.14, bf16[5,384,128]{2,1,0:T(8,128)(2,1)S(1)} %get-tuple-element.69.refs_2_, ...), custom_call_target="tpu_custom_call" | custom-call | flops 1000000000 | bytes 1 | tf_op jit(solution)/shard_map/assemble/pallas_call | solution.py:200
  69.2 4.0 %collective-permute-done.8.first_ref = bf16[5,384,128]{2,1,0:T(8,128)(2,1)} collective-permute-done((bf16[5,384,128]{2,1,0:T(8,128)(2,1)S(1)}, bf16[5,384,128]{2,1,0:T(8,128)(2,1)}, u32[]{:S(2)}, u32[]{:S(2)}) %collective-permute-start.8) | collective-permute-done | bytes 491552 | tf_op jit(solution)/shard_map/ppermute | solution.py:258
  73.2 2.7 %complete.1 = bf16[384,40,128]{2,1,0:T(8,128)(2,1)} custom-call(s32[1]{0:T(128)} %bitcast.slot_ref, bf16[5,384,128]{2,1,0:T(8,128)(2,1)} %collective-permute-done.8.first_ref, bf16[5,384,128]{2,1,0:T(8,128)(2,1)} %collective-permute-done.13.second_ref, bf16[16,384,128]{2,1,0:T(8,128)(2,1)S(1)} %get-tuple-element.76.old_ref, ...), custom_call_target="tpu_custom_call", output_to_operand_aliasing={{}: (4, {})} | custom-call | tf_op jit(solution)/shard_map/complete/pallas_call | solution.py:241
  (54 shorter events, 10.2 us)
Async XLA Ops:
  0.0 9.5 %copy-start.9 = (f32[1,128]{1,0:T(1,128)S(1)}, f32[1,128]{1,0:T(1,128)}, u32[]{:S(2)}) copy-start(f32[1,128]{1,0:T(1,128)} %constant.36.clone.refs_2_) | copy-start | bytes 1540
  0.0 9.5 %copy-start = (bf16[384,2,10,128]{3,1,2,0:T(2,128)(2,1)S(1)}, bf16[384,2,10,128]{3,1,2,0:T(2,128)(2,1)}, u32[]{:S(2)}) copy-start(bf16[384,2,10,128]{3,1,2,0:T(2,128)(2,1)} %param.7) | copy-start | bytes 5898244
  0.0 8.7 %copy-start.7 = (s32[384]{0:T(512)S(1)}, s32[384]{0:T(512)}, u32[]{:S(2)}) copy-start(s32[384]{0:T(512)} %param.9) | copy-start | bytes 4612
  0.0 8.7 %copy-start.8 = (s32[384]{0:T(512)S(1)}, s32[384]{0:T(512)}, u32[]{:S(2)}) copy-start(s32[384]{0:T(512)} %param.8) | copy-start | bytes 4612
  0.0 32.2 %collective-permute-start.4 = (bf16[384,2,10,128]{3,1,2,0:T(2,128)(2,1)}, bf16[384,2,10,128]{3,1,2,0:T(2,128)(2,1)}, u32[]{:S(2)}, u32[]{:S(2)}) collective-permute-start(bf16[384,2,10,128]{3,1,2,0:T(2,128)(2,1)} %param.7), channel_id=1, source_target_pairs={{0,1},{1,2},{2,3},{3,4},{4,5},{5,6},{6,7},{7,0},{8,9},{9,10},{10,1... | collective-permute-start | bytes 5898248 | tf_op jit(solution)/shard_map/ppermute | solution.py:23
  6.2 23.0 %collective-permute-start.2 = (bf16[384,2,5,128]{3,1,2,0:T(2,128)(2,1)}, bf16[384,2,5,128]{3,1,2,0:T(2,128)(2,1)}, u32[]{:S(2)}, u32[]{:S(2)}) collective-permute-start(bf16[384,2,5,128]{3,1,2,0:T(2,128)(2,1)} %get-tuple-element.80), channel_id=1, source_target_pairs={{0,8},{8,0},{16,24},{24,16},{1,9},{9,1},{17,25},{25,17},{2,10},{10... | collective-permute-start | bytes 2949128 | tf_op jit(solution)/shard_map/ppermute | solution.py:258
  7.5 24.1 %collective-permute-start.3 = (bf16[384,2,5,128]{3,1,2,0:T(2,128)(2,1)}, bf16[384,2,5,128]{3,1,2,0:T(2,128)(2,1)}, u32[]{:S(2)}, u32[]{:S(2)}) collective-permute-start(bf16[384,2,5,128]{3,1,2,0:T(2,128)(2,1)} %get-tuple-element.79), channel_id=1, source_target_pairs={{0,16},{16,0},{8,24},{24,8},{1,17},{17,1},{9,25},{25,9},{2,18},{18... | collective-permute-start | bytes 2949128 | tf_op jit(solution)/shard_map/ppermute | solution.py:258
  8.7 15.9 %collective-permute-start = (s32[2,384]{1,0:T(2,128)S(1)}, s32[2,384]{1,0:T(2,128)S(1)}, u32[]{:S(2)}, u32[]{:S(2)}) collective-permute-start(s32[2,384]{1,0:T(2,128)S(1)} %pad_add_fusion), channel_id=1, source_target_pairs={{0,1},{1,2},{2,3},{3,4},{4,5},{5,6},{6,7},{7,0},{8,9},{9,10},{10,1... | collective-permute-start | bytes 9224 | tf_op jit(solution)/shard_map/ppermute | solution.py:23
  19.4 22.6 %collective-permute-start.6 = (bf16[5,384,128]{2,1,0:T(8,128)(2,1)}, bf16[5,384,128]{2,1,0:T(8,128)(2,1)}, u32[]{:S(2)}, u32[]{:S(2)}) collective-permute-start(bf16[5,384,128]{2,1,0:T(8,128)(2,1)} %get-tuple-element.44), channel_id=1, source_target_pairs={{0,16},{16,0},{8,24},{24,8},{1,17},{17,1},{9,25},{25,9},{2,18},{18... | collective-permute-start | bytes 1474568 | tf_op jit(solution)/shard_map/ppermute | solution.py:258
  24.6 17.3 %collective-permute-start.7 = (bf16[5,384,128]{2,1,0:T(8,128)(2,1)}, bf16[5,384,128]{2,1,0:T(8,128)(2,1)}, u32[]{:S(2)}, u32[]{:S(2)}) collective-permute-start(bf16[5,384,128]{2,1,0:T(8,128)(2,1)} %get-tuple-element.47), channel_id=1, source_target_pairs={{0,8},{8,0},{16,24},{24,16},{1,9},{9,1},{17,25},{25,17},{2,10},{10... | collective-permute-start | bytes 1474568 | tf_op jit(solution)/shard_map/ppermute | solution.py:258
  29.2 23.4 %collective-permute-start.1 = (bf16[5,384,128]{2,1,0:T(8,128)(2,1)}, bf16[5,384,128]{2,1,0:T(8,128)(2,1)S(1)}, u32[]{:S(2)}, u32[]{:S(2)}) collective-permute-start(bf16[5,384,128]{2,1,0:T(8,128)(2,1)} %get-tuple-element.43), channel_id=1, source_target_pairs={{0,16},{16,0},{8,24},{24,8},{1,17},{17,1},{9,25},{25,9},{2,18},{18... | collective-permute-start | bytes 1474568 | tf_op jit(solution)/shard_map/ppermute | solution.py:258
  31.5 24.4 %collective-permute-start.9 = (bf16[5,384,128]{2,1,0:T(8,128)(2,1)}, bf16[5,384,128]{2,1,0:T(8,128)(2,1)S(1)}, u32[]{:S(2)}, u32[]{:S(2)}) collective-permute-start(bf16[5,384,128]{2,1,0:T(8,128)(2,1)} %get-tuple-element.63), channel_id=1, source_target_pairs={{0,8},{8,0},{16,24},{24,16},{1,9},{9,1},{17,25},{25,17},{2,10},{10... | collective-permute-start | bytes 1474568 | tf_op jit(solution)/shard_map/ppermute | solution.py:258
  32.2 16.9 %collective-permute-start.5 = (bf16[384,2,5,128]{3,1,2,0:T(2,128)(2,1)}, bf16[384,2,5,128]{3,1,2,0:T(2,128)(2,1)S(1)}, u32[]{:S(2)}, u32[]{:S(2)}) collective-permute-start(bf16[384,2,5,128]{3,1,2,0:T(2,128)(2,1)} %collective-permute-done.2), channel_id=1, source_target_pairs={{0,1},{1,2},{2,3},{3,4},{4,5},{5,6},{6,7},{7,0},{8,9},{9,10},{10,1... | collective-permute-start | bytes 2949128 | tf_op jit(solution)/shard_map/ppermute | solution.py:23
  33.9 9.2 %copy-start.2 = (bf16[2,10,384,128]{3,2,1,0:T(8,128)(2,1)S(1)}, bf16[2,10,384,128]{3,2,1,0:T(8,128)(2,1)}, u32[]{:S(2)}) copy-start(bf16[2,10,384,128]{3,2,1,0:T(8,128)(2,1)} %copy-done.1) | copy-start | bytes 5898244
  39.3 13.8 %copy-start.3 = (bf16[2,5,384,128]{3,2,1,0:T(8,128)(2,1)}, bf16[2,5,384,128]{3,2,1,0:T(8,128)(2,1)S(1)}, u32[]{:S(2)}) copy-start(bf16[2,5,384,128]{3,2,1,0:T(8,128)(2,1)S(1)} %get-tuple-element.50) | copy-start | bytes 2949124
  39.3 17.1 %copy-start.5 = (bf16[2,5,384,128]{3,2,1,0:T(8,128)(2,1)}, bf16[2,5,384,128]{3,2,1,0:T(8,128)(2,1)S(1)}, u32[]{:S(2)}) copy-start(bf16[2,5,384,128]{3,2,1,0:T(8,128)(2,1)S(1)} %get-tuple-element.66) | copy-start | bytes 2949124
  42.0 14.0 %collective-permute-start.10 = (bf16[384,2,5,128]{3,1,2,0:T(2,128)(2,1)}, bf16[384,2,5,128]{3,1,2,0:T(2,128)(2,1)S(1)}, u32[]{:S(2)}, u32[]{:S(2)}) collective-permute-start(bf16[384,2,5,128]{3,1,2,0:T(2,128)(2,1)} %collective-permute-done.3), channel_id=1, source_target_pairs={{0,1},{1,2},{2,3},{3,4},{4,5},{5,6},{6,7},{7,0},{8,9},{9,10},{10,1... | collective-permute-start | bytes 2949128 | tf_op jit(solution)/shard_map/ppermute | solution.py:23
  47.9 16.3 %collective-permute-start.11 = (bf16[5,384,128]{2,1,0:T(8,128)(2,1)}, bf16[5,384,128]{2,1,0:T(8,128)(2,1)}, u32[]{:S(2)}, u32[]{:S(2)}) collective-permute-start(bf16[5,384,128]{2,1,0:T(8,128)(2,1)} %get-tuple-element.54), channel_id=1, source_target_pairs={{0,16},{16,0},{8,24},{24,8},{1,17},{17,1},{9,25},{25,9},{2,18},{18... | collective-permute-start | bytes 1474568 | tf_op jit(solution)/shard_map/ppermute | solution.py:258
  49.1 15.0 %collective-permute-start.12 = (bf16[5,384,128]{2,1,0:T(8,128)(2,1)}, bf16[5,384,128]{2,1,0:T(8,128)(2,1)}, u32[]{:S(2)}, u32[]{:S(2)}) collective-permute-start(bf16[5,384,128]{2,1,0:T(8,128)(2,1)} %get-tuple-element.72), channel_id=1, source_target_pairs={{0,8},{8,0},{16,24},{24,16},{1,9},{9,1},{17,25},{25,17},{2,10},{10... | collective-permute-start | bytes 1474568 | tf_op jit(solution)/shard_map/ppermute | solution.py:258
  52.2 2.4 %copy-start.13 = (bf16[5,384,128]{2,1,0:T(8,128)(2,1)}, bf16[5,384,128]{2,1,0:T(8,128)(2,1)S(1)}, u32[]{:S(2)}) copy-start(bf16[5,384,128]{2,1,0:T(8,128)(2,1)S(1)} %get-tuple-element.61.refs_1_) | copy-start | bytes 1474564
  54.6 18.6 %collective-permute-start.8 = (bf16[5,384,128]{2,1,0:T(8,128)(2,1)S(1)}, bf16[5,384,128]{2,1,0:T(8,128)(2,1)}, u32[]{:S(2)}, u32[]{:S(2)}) collective-permute-start(bf16[5,384,128]{2,1,0:T(8,128)(2,1)S(1)} %attend.7), channel_id=1, source_target_pairs={{0,16},{16,0},{8,24},{24,8},{1,17},{17,1},{9,25},{25,9},{2,18},{18... | collective-permute-start | bytes 1474568 | tf_op jit(solution)/shard_map/ppermute | solution.py:258
  58.7 14.5 %collective-permute-start.13 = (bf16[5,384,128]{2,1,0:T(8,128)(2,1)}, bf16[5,384,128]{2,1,0:T(8,128)(2,1)}, u32[]{:S(2)}, u32[]{:S(2)}) collective-permute-start(bf16[5,384,128]{2,1,0:T(8,128)(2,1)} %attend.8), channel_id=1, source_target_pairs={{0,8},{8,0},{16,24},{24,16},{1,9},{9,1},{17,25},{25,17},{2,10},{10... | collective-permute-start | bytes 1474568 | tf_op jit(solution)/shard_map/ppermute | solution.py:258
  61.5 2.7 %copy-start.12 = (bf16[5,384,128]{2,1,0:T(8,128)(2,1)S(1)}, bf16[5,384,128]{2,1,0:T(8,128)(2,1)}, u32[]{:S(2)}) copy-start(bf16[5,384,128]{2,1,0:T(8,128)(2,1)} %copy-done.11) | copy-start | bytes 1474564
  61.5 2.7 %copy-start.14 = (bf16[5,384,128]{2,1,0:T(8,128)(2,1)S(1)}, bf16[5,384,128]{2,1,0:T(8,128)(2,1)}, u32[]{:S(2)}) copy-start(bf16[5,384,128]{2,1,0:T(8,128)(2,1)} %copy-done.13) | copy-start | bytes 1474564
  (5 other events, 6.6 us)

commit v4 on v3

--- a/solution.py
+++ b/solution.py
@@ -213,23 +213,30 @@
     )(slots, *pieces)
 
 
-def complete(gathered, old, pieces, slot):
+def complete(gathered, old, pieces):
     count, tokens, head_dim = pieces[0].shape
     mine = 2 * count
     window = old.shape[0]
 
     steps = tokens // BLOCK
 
-    def kernel(slot_ref, first_ref, second_ref, old_ref, _, out_ref, placed, ready, sems):
-        block = (slot_ref[0] * mine) // ROWS
-        low = slot_ref[0] * mine - block * ROWS
+    def kernel(first_ref, second_ref, old_ref, _, out_ref, landed, placed, ready, load_sems, sems):
+        loads = []
+        for i in range(steps):
+            at = pl.ds(i * BLOCK, BLOCK)
+            loads.append(pltpu.make_async_copy(second_ref.at[:, at], landed.at[i], load_sems.at[i]))
+            loads[i].start()
+        first_head = (lax.axis_index("section") ^ 3) * mine
+        block = first_head // ROWS
+        low = first_head - block * ROWS
         placed[...] = old_ref[...]
         placed[pl.ds(low, count)] = first_ref[...]
-        placed[pl.ds(low + count, count)] = second_ref[...]
         heads_at = pl.ds(pl.multiple_of(block * ROWS, ROWS), window)
         copies = []
         for i in range(steps):
             at = slice(i * BLOCK, (i + 1) * BLOCK)
+            loads[i].wait()
+            placed[pl.ds(low + count, count), at] = landed[i]
             ready[at] = jnp.swapaxes(placed[:, at], 0, 1)
             at = pl.ds(i * BLOCK, BLOCK)
             copies.append(pltpu.make_async_copy(ready.at[at], out_ref.at[at, heads_at], sems.at[i]))
@@ -240,18 +247,20 @@
     anywhere = pl.BlockSpec(memory_space=pl.ANY)
     return pl.pallas_call(
         kernel,
-        in_specs=[IN_SMEM, IN_VMEM, IN_VMEM, IN_VMEM, anywhere],
+        in_specs=[IN_VMEM, anywhere, IN_VMEM, anywhere],
         out_specs=anywhere,
         out_shape=jax.ShapeDtypeStruct(gathered.shape, gathered.dtype),
         scratch_shapes=[
+            pltpu.VMEM((steps, count, BLOCK, head_dim), jnp.bfloat16),
             pltpu.VMEM((window, tokens, head_dim), jnp.bfloat16),
             pltpu.VMEM((tokens, window, head_dim), jnp.bfloat16),
             pltpu.SemaphoreType.DMA((steps,)),
+            pltpu.SemaphoreType.DMA((steps,)),
         ],
-        input_output_aliases={4: 0},
+        input_output_aliases={3: 0},
         compiler_params=PARAMS,
         name="complete",
-    )(slot, *pieces, old, gathered)
+    )(*pieces, old, gathered)
 
 
 def across(value, route):
@@ -339,7 +348,7 @@
     gathered, old = assemble(pieces, slots, queries.shape[2], start.astype(jnp.int32), window)
     back_far_a = after(back_far_a, gathered)
     back_far_b = after(back_far_b, back_far_a)
-    return complete(gathered, old, (back_far_a, back_far_b), opposite[None].astype(jnp.int32))[None]
+    return complete(gathered, old, (back_far_a, back_far_b))[None]
 
 
 def general_body(queries, keys_values, positions, documents):

time: 76.8 us -> 76.4 us (level)
    pallas_call x5, Pallas kernels: 14.1 us -> 14.9 us  [attend(): pl.pallas_call(kernel, in_specs=[IN_VMEM] * (2 + 3 * n), out_specs=[IN_VM...]
  transfers between devices with their start and end apart: 14 -> 14, of which waited for: 6 -> 6; matrix products, arithmetic and copies ran while one was open for 5% -> 5% of each run, Pallas kernels for 42% -> 43%
where the time goes in v4:
time: 76.4 us; the launch traced here: 75.7 us
  Pallas kernels  35 us (46%)
  starting transfers between devices  15.6 us (20%)
  waiting for transfers between devices  15.3 us (20%)
  local copies, waits for them, and re-layouts  9.49 us (12%)
    pallas_call x5, Pallas kernels, attend(): pl.pallas_call(kernel, in_specs=[IN_VMEM] * (2 + 3 * n), out_specs=[IN_VM...  14.9 us
    ppermute x10, waiting for transfers between devices, across(): return lax.ppermute(value, 'section', route)  10.2 us
    ppermute x10, starting transfers between devices, across(): return lax.ppermute(value, 'section', route)  9.35 us
    pallas_call x5, Pallas kernels, prepare_cache(): pl.pallas_call(kernel, in_specs=[IN_VMEM] * (len(rows) + 2), out_specs=[I...  7.64 us
    ppermute x4, starting transfers between devices, shifted(): return lax.ppermute(block, axis, [(i, (i + 1) % size) for i in range(size)])  6.24 us
    unnamed x30, local copies, waits for them, and re-layouts  5.83 us
    pallas_call x1, Pallas kernels, prepare_queries(): pl.pallas_call(kernel, in_specs=[IN_SMEM] + [IN_VMEM] * 3, out_specs=[IN_...  5.06 us
    pallas_call x1, Pallas kernels, assemble(): pl.pallas_call(kernel, grid_spec=pltpu.PrefetchScalarGridSpec(num_scalar_...  5.05 us
  transfers between devices with their start and end apart: 14, of which 6 were waited for; matrix products, arithmetic and copies ran while one was open for 5% of the time, Pallas kernels for 43%

profile of v4, /device:TPU:1, one launch (start us, length us, event | category | flops | bytes accessed | tf_op | source)
XLA Modules:
  0.0 75.7 jit_solution(9351953190926635594)
XLA Ops:
  0.0 2.7 %collective-permute-start.4 = (bf16[384,2,10,128]{3,1,2,0:T(2,128)(2,1)}, bf16[384,2,10,128]{3,1,2,0:T(2,128)(2,1)}, u32[]{:S(2)}, u32[]{:S(2)}) collective-permute-start(bf16[384,2,10,128]{3,1,2,0:T(2,128)(2,1)} %param.7), channel_id=1, source_target_pairs={{0,1},{1,2},{2,3},{3,4},{4,5},{5,6},{6,7},{7,0},{8,9},{9,10},{10,1... | collective-permute-start | bytes 5898248 | tf_op jit(solution)/shard_map/ppermute | solution.py:23
  2.8 3.5 %fusion.1 = (bf16[384,2,5,128]{3,1,2,0:T(2,128)(2,1)}, bf16[384,2,5,128]{3,1,2,0:T(2,128)(2,1)}) fusion(bf16[384,2,10,128]{3,1,2,0:T(2,128)(2,1)} %param.7), kind=kLoop, calls=%fused_computation.4 | loop fusion | bytes 3932160 | tf_op jit(solution)/shard_map/slice | solution.py:283
  7.5 1.2 %collective-permute-start.3 = (bf16[384,2,5,128]{3,1,2,0:T(2,128)(2,1)}, bf16[384,2,5,128]{3,1,2,0:T(2,128)(2,1)}, u32[]{:S(2)}, u32[]{:S(2)}) collective-permute-start(bf16[384,2,5,128]{3,1,2,0:T(2,128)(2,1)} %get-tuple-element.79), channel_id=1, source_target_pairs={{0,16},{16,0},{8,24},{24,8},{1,17},{17,1},{9,25},{25,9},{2,18},{18... | collective-permute-start | bytes 2949128 | tf_op jit(solution)/shard_map/ppermute | solution.py:267
  9.5 1.3 %prepare_cache.5 = (bf16[2,10,384,128]{3,2,1,0:T(8,128)(2,1)S(1)}, f32[384,128]{1,0:T(8,128)S(1)}, f32[384,128]{1,0:T(8,128)S(1)}) custom-call(bf16[7680,128]{1,0:T(8,128)(2,1)S(1)} %bitcast.48, s32[3,128]{1,0:T(4,128)S(1)} %bitcast.73, f32[1,128]{1,0:T(1,128)S(1)} %copy-done.9), custom_call_target="tpu_custom_call" | custom-call | flops 1 | bytes 1 | tf_op jit(solution)/shard_map/prepare_cache/pallas_call | solution.py:82
  10.9 1.3 %copy-done.1 = bf16[2,10,384,128]{3,2,1,0:T(8,128)(2,1)} copy-done((bf16[2,10,384,128]{3,2,1,0:T(8,128)(2,1)}, bf16[2,10,384,128]{3,2,1,0:T(8,128)(2,1)S(1)}, u32[]{:S(2)}) %copy-start.1) | copy-done | bytes 1966104
  12.2 2.1 %copy-done.10 = bf16[1,384,40,128]{3,2,1,0:T(8,128)(2,1)S(1)} copy-done((bf16[1,384,40,128]{3,2,1,0:T(8,128)(2,1)S(1)}, bf16[1,384,40,128]{3,2,1,0:T(8,128)(2,1)}, u32[]{:S(2)}) %copy-start.10) | copy-done | bytes 3932184
  14.3 5.1 %prepare_queries.1 = (bf16[5,384,128]{2,1,0:T(8,128)(2,1)}, bf16[5,384,128]{2,1,0:T(8,128)(2,1)}, bf16[5,384,128]{2,1,0:T(8,128)(2,1)}, bf16[5,384,128]{2,1,0:T(...) custom-call(s32[7]{0:T(128)S(1)} %stack.61.starts_ref, ...), custom_call_target="tpu_custom_call" | custom-call | flops 2000000000 | bytes 7864320 | tf_op jit(solution)/shard_map/prepare_queries/pallas_call | solution.py:111
  19.6 5.0 %collective-permute-done = s32[2,384]{1,0:T(2,128)S(1)} collective-permute-done((s32[2,384]{1,0:T(2,128)S(1)}, s32[2,384]{1,0:T(2,128)S(1)}, u32[]{:S(2)}, u32[]{:S(2)}) %collective-permute-start) | collective-permute-done | bytes 3104 | tf_op jit(solution)/shard_map/ppermute | solution.py:23
  25.9 3.4 %collective-permute-done.2 = bf16[384,2,5,128]{3,1,2,0:T(2,128)(2,1)} collective-permute-done((bf16[384,2,5,128]{3,1,2,0:T(2,128)(2,1)}, bf16[384,2,5,128]{3,1,2,0:T(2,128)(2,1)}, u32[]{:S(2)}, u32[]{:S(2)}) %collective-permute-start.2) | collective-permute-done | bytes 983072 | tf_op jit(solution)/shard_map/ppermute | solution.py:267
  29.2 1.8 %collective-permute-start.1 = (bf16[5,384,128]{2,1,0:T(8,128)(2,1)}, bf16[5,384,128]{2,1,0:T(8,128)(2,1)S(1)}, u32[]{:S(2)}, u32[]{:S(2)}) collective-permute-start(bf16[5,384,128]{2,1,0:T(8,128)(2,1)} %get-tuple-element.43), channel_id=1, source_target_pairs={{0,16},{16,0},{8,24},{24,8},{1,17},{17,1},{9,25},{25,9},{2,18},{18... | collective-permute-start | bytes 1474568 | tf_op jit(solution)/shard_map/ppermute | solution.py:267
  32.2 1.6 %collective-permute-start.5 = (bf16[384,2,5,128]{3,1,2,0:T(2,128)(2,1)}, bf16[384,2,5,128]{3,1,2,0:T(2,128)(2,1)S(1)}, u32[]{:S(2)}, u32[]{:S(2)}) collective-permute-start(bf16[384,2,5,128]{3,1,2,0:T(2,128)(2,1)} %collective-permute-done.2), channel_id=1, source_target_pairs={{0,1},{1,2},{2,3},{3,4},{4,5},{5,6},{6,7},{7,0},{8,9},{9,10},{10,1... | collective-permute-start | bytes 2949128 | tf_op jit(solution)/shard_map/ppermute | solution.py:23
  33.9 3.1 %prepare_cache.6 = (bf16[2,10,384,128]{3,2,1,0:T(8,128)(2,1)S(1)}, f32[384,128]{1,0:T(8,128)S(1)}, f32[384,128]{1,0:T(8,128)S(1)}) custom-call(bf16[7680,128]{1,0:T(8,128)(2,1)} %bitcast.13.refs_0_, s32[3,128]{1,0:T(4,128)S(1)} %bitcast.74, f32[1,128]{1,0:T(1,128)S(1)} %copy-done.9), custom_call_target="tpu_custom_call" | custom-call | flops 1 | bytes 1 | tf_op jit(solution)/shard_map/prepare_cache/pallas_call | solution.py:82
  36.9 2.3 %prepare_cache.7 = (bf16[2,5,384,128]{3,2,1,0:T(8,128)(2,1)S(1)}, bf16[2,5,384,128]{3,2,1,0:T(8,128)(2,1)S(1)}) custom-call(bf16[3840,128]{1,0:T(8,128)(2,1)} %bitcast.15.refs_0_, bf16[3840,128]{1,0:T(8,128)(2,1)} %bitcast.17.refs_1_, f32[384,128]{1,0:T(8,128)S(1)} %get-tuple-element.41.cosine_ref.refs_2_, f32[384,128]{1,0:T(8,128)S(1)} %get-tuple-element.42.sine_ref.refs_3_), custom_call_target="tpu_custom_call" | custom-call | flops 1 | bytes 1 | tf_op jit(solution)/shard_map/prepare_cache/pallas_call | solution.py:82
  39.3 2.7 %collective-permute-done.6.refs_0_ = bf16[5,384,128]{2,1,0:T(8,128)(2,1)} collective-permute-done((bf16[5,384,128]{2,1,0:T(8,128)(2,1)}, bf16[5,384,128]{2,1,0:T(8,128)(2,1)}, u32[]{:S(2)}, u32[]{:S(2)}) %collective-permute-start.6) | collective-permute-done | bytes 491552 | tf_op jit(solution)/shard_map/ppermute | solution.py:267
  43.1 4.8 %attend.5 = (bf16[5,384,128]{2,1,0:T(8,128)(2,1)}, bf16[5,384,128]{2,1,0:T(8,128)(2,1)}) custom-call(s32[3,128]{1,0:T(4,128)S(1)} %bitcast.63, s32[3,128]{1,0:T(4,128)S(1)} %bitcast.68, bf16[5,384,128]{2,1,0:T(8,128)(2,1)} %collective-permute-done.6.refs_0_, bf16[7680,128]{1,0:T(8,128)(2,1)S(1)} %bitcast.49, bf16[7680,128]{1,0:T(8,128)(2,1)S(1)} %bitcast.53, ...), custom_call_target="tpu_custom_call" | custom-call | flops 49999998976 | bytes 1 | tf_op jit(solution)/shard_map/attend/pallas_call | solution.py:168
  47.9 1.2 %collective-permute-start.11 = (bf16[5,384,128]{2,1,0:T(8,128)(2,1)}, bf16[5,384,128]{2,1,0:T(8,128)(2,1)}, u32[]{:S(2)}, u32[]{:S(2)}) collective-permute-start(bf16[5,384,128]{2,1,0:T(8,128)(2,1)} %get-tuple-element.54), channel_id=1, source_target_pairs={{0,16},{16,0},{8,24},{24,8},{1,17},{17,1},{9,25},{25,9},{2,18},{18... | collective-permute-start | bytes 1474568 | tf_op jit(solution)/shard_map/ppermute | solution.py:267
  49.4 2.8 %attend.6 = (bf16[5,384,128]{2,1,0:T(8,128)(2,1)S(1)}, bf16[5,384,128]{2,1,0:T(8,128)(2,1)S(1)}) custom-call(s32[3,128]{1,0:T(4,128)S(1)} %bitcast.64, s32[3,128]{1,0:T(4,128)S(1)} %bitcast.69, bf16[10,384,128]{2,1,0:T(8,128)(2,1)S(1)} %get-tuple-element.55.refs_0_.refs_3_, bf16[7680,128]{1,0:T(8,128)(2,1)S(1)} %bitcast.51, bf16[7680,128]{1,0:T(8,128)(2,1)S(1)} %bitcast.55, ...), custom_call_target="tpu_custom_call" | custom-call | flops 1 | bytes 1 | tf_op jit(solution)/shard_map/attend/pallas_call | solution.py:168
  53.1 2.3 %attend.7 = bf16[5,384,128]{2,1,0:T(8,128)(2,1)} custom-call(s32[3,128]{1,0:T(4,128)S(1)} %bitcast.65, s32[3,128]{1,0:T(4,128)S(1)} %bitcast.70, bf16[5,384,128]{2,1,0:T(8,128)(2,1)S(1)} %collective-permute-done.1.refs_0_, bf16[3840,128]{1,0:T(8,128)(2,1)S(1)} %bitcast.57, bf16[3840,128]{1,0:T(8,128)(2,1)S(1)} %bitcast.44), custom_call_target="tpu_custom_call" | custom-call | flops 1 | bytes 1 | tf_op jit(solution)/shard_map/attend/pallas_call | solution.py:168
  55.4 1.2 %collective-permute-start.8 = (bf16[5,384,128]{2,1,0:T(8,128)(2,1)}, bf16[5,384,128]{2,1,0:T(8,128)(2,1)S(1)}, u32[]{:S(2)}, u32[]{:S(2)}) collective-permute-start(bf16[5,384,128]{2,1,0:T(8,128)(2,1)} %attend.7), channel_id=1, source_target_pairs={{0,16},{16,0},{8,24},{24,8},{1,17},{17,1},{9,25},{25,9},{2,18},{18... | collective-permute-start | bytes 1474568 | tf_op jit(solution)/shard_map/ppermute | solution.py:267
  57.1 2.3 %attend.8 = bf16[5,384,128]{2,1,0:T(8,128)(2,1)} custom-call(s32[3,128]{1,0:T(4,128)S(1)} %bitcast.66, s32[3,128]{1,0:T(4,128)S(1)} %bitcast.71, bf16[5,384,128]{2,1,0:T(8,128)(2,1)S(1)} %collective-permute-done.9.refs_0_, bf16[3840,128]{1,0:T(8,128)(2,1)S(1)} %bitcast.59, bf16[3840,128]{1,0:T(8,128)(2,1)S(1)} %bitcast.46), custom_call_target="tpu_custom_call" | custom-call | flops 1 | bytes 1 | tf_op jit(solution)/shard_map/attend/pallas_call | solution.py:168
  62.2 2.7 %attend.9 = (bf16[5,384,128]{2,1,0:T(8,128)(2,1)S(1)}, bf16[5,384,128]{2,1,0:T(8,128)(2,1)S(1)}) custom-call(s32[3,128]{1,0:T(4,128)S(1)} %bitcast.67, s32[3,128]{1,0:T(4,128)S(1)} %bitcast.72, bf16[10,384,128]{2,1,0:T(8,128)(2,1)S(1)} %get-tuple-element.68.refs_0_.refs_3_, bf16[3840,128]{1,0:T(8,128)(2,1)S(1)} %bitcast.58, bf16[3840,128]{1,0:T(8,128)(2,1)S(1)} %bitcast.45, ...), custom_call_target="tpu_custom_call" | custom-call | flops 1 | bytes 1 | tf_op jit(solution)/shard_map/attend/pallas_call | solution.py:168
  64.9 5.0 %assemble.1 = (bf16[384,40,128]{2,1,0:T(8,128)(2,1)}, bf16[16,384,128]{2,1,0:T(8,128)(2,1)S(1)}) custom-call(s32[7]{0:T(128)S(1)} %concatenate.3.slots_ref, bf16[5,384,128]{2,1,0:T(8,128)(2,1)S(1)} %copy-done.12, bf16[5,384,128]{2,1,0:T(8,128)(2,1)S(1)} %copy-done.14, bf16[5,384,128]{2,1,0:T(8,128)(2,1)S(1)} %get-tuple-element.69.refs_2_, ...), custom_call_target="tpu_custom_call" | custom-call | flops 1000000000 | bytes 1 | tf_op jit(solution)/shard_map/assemble/pallas_call | solution.py:200
  69.9 3.3 %collective-permute-done.8.first_ref = bf16[5,384,128]{2,1,0:T(8,128)(2,1)S(1)} collective-permute-done((bf16[5,384,128]{2,1,0:T(8,128)(2,1)}, bf16[5,384,128]{2,1,0:T(8,128)(2,1)S(1)}, u32[]{:S(2)}, u32[]{:S(2)}) %collective-permute-start.8) | collective-permute-done | bytes 491552 | tf_op jit(solution)/shard_map/ppermute | solution.py:267
  73.2 2.4 %complete.1 = bf16[384,40,128]{2,1,0:T(8,128)(2,1)} custom-call(bf16[5,384,128]{2,1,0:T(8,128)(2,1)S(1)} %collective-permute-done.8.first_ref, bf16[5,384,128]{2,1,0:T(8,128)(2,1)} %collective-permute-done.13.second_ref, bf16[16,384,128]{2,1,0:T(8,128)(2,1)S(1)} %get-tuple-element.76.old_ref, ...), custom_call_target="tpu_custom_call", output_to_operand_aliasing={{}: (3, {})} | custom-call | tf_op jit(solution)/shard_map/complete/pallas_call | solution.py:248
  (54 shorter events, 10.2 us)
Async XLA Ops:
  0.0 9.5 %copy-start.9 = (f32[1,128]{1,0:T(1,128)S(1)}, f32[1,128]{1,0:T(1,128)}, u32[]{:S(2)}) copy-start(f32[1,128]{1,0:T(1,128)} %constant.36.clone.refs_2_) | copy-start | bytes 1540
  0.0 9.5 %copy-start = (bf16[384,2,10,128]{3,1,2,0:T(2,128)(2,1)S(1)}, bf16[384,2,10,128]{3,1,2,0:T(2,128)(2,1)}, u32[]{:S(2)}) copy-start(bf16[384,2,10,128]{3,1,2,0:T(2,128)(2,1)} %param.7) | copy-start | bytes 5898244
  0.0 8.7 %copy-start.7 = (s32[384]{0:T(512)S(1)}, s32[384]{0:T(512)}, u32[]{:S(2)}) copy-start(s32[384]{0:T(512)} %param.9) | copy-start | bytes 4612
  0.0 8.7 %copy-start.8 = (s32[384]{0:T(512)S(1)}, s32[384]{0:T(512)}, u32[]{:S(2)}) copy-start(s32[384]{0:T(512)} %param.8) | copy-start | bytes 4612
  0.0 32.2 %collective-permute-start.4 = (bf16[384,2,10,128]{3,1,2,0:T(2,128)(2,1)}, bf16[384,2,10,128]{3,1,2,0:T(2,128)(2,1)}, u32[]{:S(2)}, u32[]{:S(2)}) collective-permute-start(bf16[384,2,10,128]{3,1,2,0:T(2,128)(2,1)} %param.7), channel_id=1, source_target_pairs={{0,1},{1,2},{2,3},{3,4},{4,5},{5,6},{6,7},{7,0},{8,9},{9,10},{10,1... | collective-permute-start | bytes 5898248 | tf_op jit(solution)/shard_map/ppermute | solution.py:23
  6.2 23.0 %collective-permute-start.2 = (bf16[384,2,5,128]{3,1,2,0:T(2,128)(2,1)}, bf16[384,2,5,128]{3,1,2,0:T(2,128)(2,1)}, u32[]{:S(2)}, u32[]{:S(2)}) collective-permute-start(bf16[384,2,5,128]{3,1,2,0:T(2,128)(2,1)} %get-tuple-element.80), channel_id=1, source_target_pairs={{0,8},{8,0},{16,24},{24,16},{1,9},{9,1},{17,25},{25,17},{2,10},{10... | collective-permute-start | bytes 2949128 | tf_op jit(solution)/shard_map/ppermute | solution.py:267
  7.5 24.1 %collective-permute-start.3 = (bf16[384,2,5,128]{3,1,2,0:T(2,128)(2,1)}, bf16[384,2,5,128]{3,1,2,0:T(2,128)(2,1)}, u32[]{:S(2)}, u32[]{:S(2)}) collective-permute-start(bf16[384,2,5,128]{3,1,2,0:T(2,128)(2,1)} %get-tuple-element.79), channel_id=1, source_target_pairs={{0,16},{16,0},{8,24},{24,8},{1,17},{17,1},{9,25},{25,9},{2,18},{18... | collective-permute-start | bytes 2949128 | tf_op jit(solution)/shard_map/ppermute | solution.py:267
  8.7 15.9 %collective-permute-start = (s32[2,384]{1,0:T(2,128)S(1)}, s32[2,384]{1,0:T(2,128)S(1)}, u32[]{:S(2)}, u32[]{:S(2)}) collective-permute-start(s32[2,384]{1,0:T(2,128)S(1)} %pad_add_fusion), channel_id=1, source_target_pairs={{0,1},{1,2},{2,3},{3,4},{4,5},{5,6},{6,7},{7,0},{8,9},{9,10},{10,1... | collective-permute-start | bytes 9224 | tf_op jit(solution)/shard_map/ppermute | solution.py:23
  19.4 22.6 %collective-permute-start.6 = (bf16[5,384,128]{2,1,0:T(8,128)(2,1)}, bf16[5,384,128]{2,1,0:T(8,128)(2,1)}, u32[]{:S(2)}, u32[]{:S(2)}) collective-permute-start(bf16[5,384,128]{2,1,0:T(8,128)(2,1)} %get-tuple-element.44), channel_id=1, source_target_pairs={{0,16},{16,0},{8,24},{24,8},{1,17},{17,1},{9,25},{25,9},{2,18},{18... | collective-permute-start | bytes 1474568 | tf_op jit(solution)/shard_map/ppermute | solution.py:267
  24.6 17.3 %collective-permute-start.7 = (bf16[5,384,128]{2,1,0:T(8,128)(2,1)}, bf16[5,384,128]{2,1,0:T(8,128)(2,1)}, u32[]{:S(2)}, u32[]{:S(2)}) collective-permute-start(bf16[5,384,128]{2,1,0:T(8,128)(2,1)} %get-tuple-element.47), channel_id=1, source_target_pairs={{0,8},{8,0},{16,24},{24,16},{1,9},{9,1},{17,25},{25,17},{2,10},{10... | collective-permute-start | bytes 1474568 | tf_op jit(solution)/shard_map/ppermute | solution.py:267
  29.2 23.4 %collective-permute-start.1 = (bf16[5,384,128]{2,1,0:T(8,128)(2,1)}, bf16[5,384,128]{2,1,0:T(8,128)(2,1)S(1)}, u32[]{:S(2)}, u32[]{:S(2)}) collective-permute-start(bf16[5,384,128]{2,1,0:T(8,128)(2,1)} %get-tuple-element.43), channel_id=1, source_target_pairs={{0,16},{16,0},{8,24},{24,8},{1,17},{17,1},{9,25},{25,9},{2,18},{18... | collective-permute-start | bytes 1474568 | tf_op jit(solution)/shard_map/ppermute | solution.py:267
  31.5 25.1 %collective-permute-start.9 = (bf16[5,384,128]{2,1,0:T(8,128)(2,1)}, bf16[5,384,128]{2,1,0:T(8,128)(2,1)S(1)}, u32[]{:S(2)}, u32[]{:S(2)}) collective-permute-start(bf16[5,384,128]{2,1,0:T(8,128)(2,1)} %get-tuple-element.63), channel_id=1, source_target_pairs={{0,8},{8,0},{16,24},{24,16},{1,9},{9,1},{17,25},{25,17},{2,10},{10... | collective-permute-start | bytes 1474568 | tf_op jit(solution)/shard_map/ppermute | solution.py:267
  32.2 16.9 %collective-permute-start.5 = (bf16[384,2,5,128]{3,1,2,0:T(2,128)(2,1)}, bf16[384,2,5,128]{3,1,2,0:T(2,128)(2,1)S(1)}, u32[]{:S(2)}, u32[]{:S(2)}) collective-permute-start(bf16[384,2,5,128]{3,1,2,0:T(2,128)(2,1)} %collective-permute-done.2), channel_id=1, source_target_pairs={{0,1},{1,2},{2,3},{3,4},{4,5},{5,6},{6,7},{7,0},{8,9},{9,10},{10,1... | collective-permute-start | bytes 2949128 | tf_op jit(solution)/shard_map/ppermute | solution.py:23
  33.9 9.2 %copy-start.2 = (bf16[2,10,384,128]{3,2,1,0:T(8,128)(2,1)S(1)}, bf16[2,10,384,128]{3,2,1,0:T(8,128)(2,1)}, u32[]{:S(2)}) copy-start(bf16[2,10,384,128]{3,2,1,0:T(8,128)(2,1)} %copy-done.1) | copy-start | bytes 5898244
  39.3 13.8 %copy-start.3 = (bf16[2,5,384,128]{3,2,1,0:T(8,128)(2,1)}, bf16[2,5,384,128]{3,2,1,0:T(8,128)(2,1)S(1)}, u32[]{:S(2)}) copy-start(bf16[2,5,384,128]{3,2,1,0:T(8,128)(2,1)S(1)} %get-tuple-element.50) | copy-start | bytes 2949124
  39.3 17.8 %copy-start.5 = (bf16[2,5,384,128]{3,2,1,0:T(8,128)(2,1)}, bf16[2,5,384,128]{3,2,1,0:T(8,128)(2,1)S(1)}, u32[]{:S(2)}) copy-start(bf16[2,5,384,128]{3,2,1,0:T(8,128)(2,1)S(1)} %get-tuple-element.66) | copy-start | bytes 2949124
  42.0 14.7 %collective-permute-start.10 = (bf16[384,2,5,128]{3,1,2,0:T(2,128)(2,1)}, bf16[384,2,5,128]{3,1,2,0:T(2,128)(2,1)S(1)}, u32[]{:S(2)}, u32[]{:S(2)}) collective-permute-start(bf16[384,2,5,128]{3,1,2,0:T(2,128)(2,1)} %collective-permute-done.3), channel_id=1, source_target_pairs={{0,1},{1,2},{2,3},{3,4},{4,5},{5,6},{6,7},{7,0},{8,9},{9,10},{10,1... | collective-permute-start | bytes 2949128 | tf_op jit(solution)/shard_map/ppermute | solution.py:23
  47.9 17.0 %collective-permute-start.11 = (bf16[5,384,128]{2,1,0:T(8,128)(2,1)}, bf16[5,384,128]{2,1,0:T(8,128)(2,1)}, u32[]{:S(2)}, u32[]{:S(2)}) collective-permute-start(bf16[5,384,128]{2,1,0:T(8,128)(2,1)} %get-tuple-element.54), channel_id=1, source_target_pairs={{0,16},{16,0},{8,24},{24,8},{1,17},{17,1},{9,25},{25,9},{2,18},{18... | collective-permute-start | bytes 1474568 | tf_op jit(solution)/shard_map/ppermute | solution.py:267
  49.1 15.7 %collective-permute-start.12 = (bf16[5,384,128]{2,1,0:T(8,128)(2,1)}, bf16[5,384,128]{2,1,0:T(8,128)(2,1)}, u32[]{:S(2)}, u32[]{:S(2)}) collective-permute-start(bf16[5,384,128]{2,1,0:T(8,128)(2,1)} %get-tuple-element.72), channel_id=1, source_target_pairs={{0,8},{8,0},{16,24},{24,16},{1,9},{9,1},{17,25},{25,17},{2,10},{10... | collective-permute-start | bytes 1474568 | tf_op jit(solution)/shard_map/ppermute | solution.py:267
  52.2 3.2 %copy-start.13 = (bf16[5,384,128]{2,1,0:T(8,128)(2,1)}, bf16[5,384,128]{2,1,0:T(8,128)(2,1)S(1)}, u32[]{:S(2)}) copy-start(bf16[5,384,128]{2,1,0:T(8,128)(2,1)S(1)} %get-tuple-element.61.refs_1_) | copy-start | bytes 1474564
  55.4 17.8 %collective-permute-start.8 = (bf16[5,384,128]{2,1,0:T(8,128)(2,1)}, bf16[5,384,128]{2,1,0:T(8,128)(2,1)S(1)}, u32[]{:S(2)}, u32[]{:S(2)}) collective-permute-start(bf16[5,384,128]{2,1,0:T(8,128)(2,1)} %attend.7), channel_id=1, source_target_pairs={{0,16},{16,0},{8,24},{24,8},{1,17},{17,1},{9,25},{25,9},{2,18},{18... | collective-permute-start | bytes 1474568 | tf_op jit(solution)/shard_map/ppermute | solution.py:267
  59.4 13.8 %collective-permute-start.13 = (bf16[5,384,128]{2,1,0:T(8,128)(2,1)}, bf16[5,384,128]{2,1,0:T(8,128)(2,1)}, u32[]{:S(2)}, u32[]{:S(2)}) collective-permute-start(bf16[5,384,128]{2,1,0:T(8,128)(2,1)} %attend.8), channel_id=1, source_target_pairs={{0,8},{8,0},{16,24},{24,16},{1,9},{9,1},{17,25},{25,17},{2,10},{10... | collective-permute-start | bytes 1474568 | tf_op jit(solution)/shard_map/ppermute | solution.py:267
  62.2 2.7 %copy-start.12 = (bf16[5,384,128]{2,1,0:T(8,128)(2,1)S(1)}, bf16[5,384,128]{2,1,0:T(8,128)(2,1)}, u32[]{:S(2)}) copy-start(bf16[5,384,128]{2,1,0:T(8,128)(2,1)} %copy-done.11) | copy-start | bytes 1474564
  62.2 2.7 %copy-start.14 = (bf16[5,384,128]{2,1,0:T(8,128)(2,1)S(1)}, bf16[5,384,128]{2,1,0:T(8,128)(2,1)}, u32[]{:S(2)}) copy-start(bf16[5,384,128]{2,1,0:T(8,128)(2,1)} %copy-done.13) | copy-start | bytes 1474564
  (5 other events, 6.6 us)
